TPU v7x, 128 devices: a whole 4x4x4 slice. The times are simulated.
128 devices in a mesh: gx: 8 (over y, z_hi), gy: 4 (over x), gz: 4 (over z_lo, core).
Axes of the slice: x: 4, y: 4, z: 4 (z_hi: 2, z_lo: 2; z = z_hi * 2 + z_lo), core: 2. Of those that a mesh axis runs over, the one named last changes fastest.
Arguments:
- concentrations: float32 [2, 256, 256, 512], P(None, 'gx', 'gy', 'gz'), may hold values from 0 to 2
- pore: int32 [256, 256, 512], P('gx', 'gy', 'gz'), may hold values 0 or 1
- permeability: float32 [256, 256, 512], P('gx', 'gy', 'gz'), may hold values from 0.85 to 1
- rate: float32 [256, 256, 512], P('gx', 'gy', 'gz'), may hold values from 0.01 to 0.1
- diffusion: float32 [2], replicated, may hold values from 0.14 to 0.16
Outputs:
- final: float32 [2, 256, 256, 512], P(None, 'gx', 'gy', 'gz')
All inputs are finite; a program needn't handle non-finite values. No bound on the sum of `pore` on one device may be relied on, other than what follows from the above.
Results may differ from a plain program's by a relative error of at most 0.00002.
Values sent between devices are 32-bit elements; how exact they have to be, the bound alone decides.
No kernel may reach another device: no remote copies, remote signals or barrier semaphores. Data moves between devices by JAX's collectives and lax.ppermute only.
A program may use at most 128 MiB of HBM per device.

v0:
```python
import jax
import jax.numpy as jnp
from jax import lax
from jax.sharding import PartitionSpec as P

STEPS = 16


def from_behind(block, axis, distance):
    devices = range(lax.axis_size(axis))
    route = [(i - distance, i) for i in devices if i - distance in devices]
    return lax.ppermute(block, axis, route)


def end_planes(fields, dim):
    count = fields.shape[dim]
    first = lax.slice_in_dim(fields, 0, 1, axis=dim)
    last = lax.slice_in_dim(fields, count - 1, count, axis=dim)
    return (first, last)


def beside(fields, dim, lower, upper):
    count = fields.shape[dim]
    place = lax.broadcasted_iota(jnp.int32, fields.shape, dim)
    down = jnp.where(place == 0, lower, jnp.roll(fields, 1, axis=dim))
    up = jnp.where(place == count - 1, upper, jnp.roll(fields, -1, axis=dim))
    return (down, up)


def faces_first(fields):
    first, last = end_planes(fields, 1)
    lower = from_behind(last, "gx", 1)
    upper = from_behind(first, "gx", -1)
    return beside(fields, 1, lower, upper)


def faces_second(fields):
    first, last = end_planes(fields, 2)
    lower = from_behind(last, "gy", 1)
    upper = from_behind(first, "gy", -1)
    return beside(fields, 2, lower, upper)


def faces_third(fields):
    first, last = end_planes(fields, 3)
    lower = from_behind(last, "gz", 1)
    upper = from_behind(first, "gz", -1)
    return beside(fields, 3, lower, upper)


def neighbours(fields):
    down_x, up_x = faces_first(fields)
    down_y, up_y = faces_second(fields)
    down_z, up_z = faces_third(fields)
    return [down_x, up_x, down_y, up_y, down_z, up_z]


def shards(concentrations, pore, permeability, rate, diffusion):
    solid = pore.astype(jnp.float32)
    rock = jnp.stack([solid * permeability, solid * rate])
    conduct = rock[0]
    react = rock[1]
    near_conduct = [item[0] for item in neighbours(rock)]

    def single_step(index, fields):
        near_fields = neighbours(fields)
        flux = jnp.zeros_like(fields)
        for near, near_k in zip(near_fields, near_conduct):
            flux = flux + near_k[None] * (near - fields)
        flux = conduct[None] * flux
        acid = fields[0]
        reacted = react * acid * acid / (1.0 + acid)
        new_acid = acid + diffusion[0] * flux[0] - reacted
        new_solute = fields[1] + diffusion[1] * flux[1] + reacted
        return jnp.stack([new_acid, new_solute])

    return lax.fori_loop(0, STEPS, single_step, concentrations)


def solution(mesh):
    placed = (
        P(None, "gx", "gy", "gz"),
        P("gx", "gy", "gz"),
        P("gx", "gy", "gz"),
        P("gx", "gy", "gz"),
        P(),
    )
    return jax.shard_map(
        shards, mesh=mesh, in_specs=placed, out_specs=P(None, "gx", "gy", "gz"), check_vma=False
    )
```

profile of v0, /device:TPU:0, one launch (start us, length us, event | category | flops | bytes accessed | tf_op | source)
XLA Modules:
  0.0 953.8 jit_solution(10284669330094979970)
XLA Ops:
  4.9 5.2 collective-permute-start.8
  33.7 6.5 collective-permute-start.6
  53.2 898.1 %while.10 = (s32[]{:T(128)}, f32[2,32,64,128]{3,1,0,2:T(8,128)S(1)}, f32[2]{0:T(128)S(1)}, f32[32,64,128]{2,0,1:T(8,128)S(1)}, f32[1,32,64,128]{3,1,2,0:T(8,128)...) while((s32[]{:T(128)}, ...), condition=%wide.region_1.2_spmd, body=%wide.region_0.1_spmd.sunk | while | flops 18874816 | bytes 70550840 | solution.py:77
  59.8 5.8 collective-permute-start.1
  67.0 7.3 collective-permute-start.5
  98.7 10.8 %fusion.67 = f32[2,32,64,128]{3,1,0,2:T(8,128)S(1)} fusion(f32[2,32,64,128]{3,1,0,2:T(8,128)S(1)} %get-tuple-element.276, f32[2,31,64,128]{3,1,0,2:T(8,128)} %get-tuple-element.241, f32[2,1,64,128]{3,1,0,2:T(1,128)S(1)} %get-tuple-element.242, f32[2,1,64,128]{3,1,0,2:T(1,128)S(1)} %get-tuple-element.243, f32[2,31,64,128]{3,1,0,2:T(8,128)} %get-tuple-element.244, ...), kind=kLoop, calls=%fused_computation.8.clone.1 | loop fusion | flops 15728640 | bytes 24347072 | tf_op jit(solution)/shard_map/while/body/eval_jaxpr/mul | solution.py:70
  123.7 6.7 collective-permute-start.5
  141.4 5.1 collective-permute-start.3
  154.7 10.8 %fusion.67 = f32[2,32,64,128]{3,1,0,2:T(8,128)S(1)} fusion(f32[2,32,64,128]{3,1,0,2:T(8,128)S(1)} %get-tuple-element.276, f32[2,31,64,128]{3,1,0,2:T(8,128)} %get-tuple-element.241, f32[2,1,64,128]{3,1,0,2:T(1,128)S(1)} %get-tuple-element.242, f32[2,1,64,128]{3,1,0,2:T(1,128)S(1)} %get-tuple-element.243, f32[2,31,64,128]{3,1,0,2:T(8,128)} %get-tuple-element.244, ...), kind=kLoop, calls=%fused_computation.8.clone.1 | loop fusion | flops 15728640 | bytes 24347072 | tf_op jit(solution)/shard_map/while/body/eval_jaxpr/mul | solution.py:70
  179.4 7.0 collective-permute-start.5
  197.3 5.1 collective-permute-start.3
  210.7 10.8 %fusion.67 = f32[2,32,64,128]{3,1,0,2:T(8,128)S(1)} fusion(f32[2,32,64,128]{3,1,0,2:T(8,128)S(1)} %get-tuple-element.276, f32[2,31,64,128]{3,1,0,2:T(8,128)} %get-tuple-element.241, f32[2,1,64,128]{3,1,0,2:T(1,128)S(1)} %get-tuple-element.242, f32[2,1,64,128]{3,1,0,2:T(1,128)S(1)} %get-tuple-element.243, f32[2,31,64,128]{3,1,0,2:T(8,128)} %get-tuple-element.244, ...), kind=kLoop, calls=%fused_computation.8.clone.1 | loop fusion | flops 15728640 | bytes 24347072 | tf_op jit(solution)/shard_map/while/body/eval_jaxpr/mul | solution.py:70
  235.3 7.0 collective-permute-start.5
  253.3 5.1 collective-permute-start.3
  266.7 10.8 %fusion.67 = f32[2,32,64,128]{3,1,0,2:T(8,128)S(1)} fusion(f32[2,32,64,128]{3,1,0,2:T(8,128)S(1)} %get-tuple-element.276, f32[2,31,64,128]{3,1,0,2:T(8,128)} %get-tuple-element.241, f32[2,1,64,128]{3,1,0,2:T(1,128)S(1)} %get-tuple-element.242, f32[2,1,64,128]{3,1,0,2:T(1,128)S(1)} %get-tuple-element.243, f32[2,31,64,128]{3,1,0,2:T(8,128)} %get-tuple-element.244, ...), kind=kLoop, calls=%fused_computation.8.clone.1 | loop fusion | flops 15728640 | bytes 24347072 | tf_op jit(solution)/shard_map/while/body/eval_jaxpr/mul | solution.py:70
  291.3 7.0 collective-permute-start.5
  309.3 5.1 collective-permute-start.3
  322.6 10.8 %fusion.67 = f32[2,32,64,128]{3,1,0,2:T(8,128)S(1)} fusion(f32[2,32,64,128]{3,1,0,2:T(8,128)S(1)} %get-tuple-element.276, f32[2,31,64,128]{3,1,0,2:T(8,128)} %get-tuple-element.241, f32[2,1,64,128]{3,1,0,2:T(1,128)S(1)} %get-tuple-element.242, f32[2,1,64,128]{3,1,0,2:T(1,128)S(1)} %get-tuple-element.243, f32[2,31,64,128]{3,1,0,2:T(8,128)} %get-tuple-element.244, ...), kind=kLoop, calls=%fused_computation.8.clone.1 | loop fusion | flops 15728640 | bytes 24347072 | tf_op jit(solution)/shard_map/while/body/eval_jaxpr/mul | solution.py:70
  347.3 7.0 collective-permute-start.5
  365.2 5.1 collective-permute-start.3
  378.6 10.8 %fusion.67 = f32[2,32,64,128]{3,1,0,2:T(8,128)S(1)} fusion(f32[2,32,64,128]{3,1,0,2:T(8,128)S(1)} %get-tuple-element.276, f32[2,31,64,128]{3,1,0,2:T(8,128)} %get-tuple-element.241, f32[2,1,64,128]{3,1,0,2:T(1,128)S(1)} %get-tuple-element.242, f32[2,1,64,128]{3,1,0,2:T(1,128)S(1)} %get-tuple-element.243, f32[2,31,64,128]{3,1,0,2:T(8,128)} %get-tuple-element.244, ...), kind=kLoop, calls=%fused_computation.8.clone.1 | loop fusion | flops 15728640 | bytes 24347072 | tf_op jit(solution)/shard_map/while/body/eval_jaxpr/mul | solution.py:70
  403.3 7.0 collective-permute-start.5
  421.2 5.1 collective-permute-start.3
  434.6 10.8 %fusion.67 = f32[2,32,64,128]{3,1,0,2:T(8,128)S(1)} fusion(f32[2,32,64,128]{3,1,0,2:T(8,128)S(1)} %get-tuple-element.276, f32[2,31,64,128]{3,1,0,2:T(8,128)} %get-tuple-element.241, f32[2,1,64,128]{3,1,0,2:T(1,128)S(1)} %get-tuple-element.242, f32[2,1,64,128]{3,1,0,2:T(1,128)S(1)} %get-tuple-element.243, f32[2,31,64,128]{3,1,0,2:T(8,128)} %get-tuple-element.244, ...), kind=kLoop, calls=%fused_computation.8.clone.1 | loop fusion | flops 15728640 | bytes 24347072 | tf_op jit(solution)/shard_map/while/body/eval_jaxpr/mul | solution.py:70
  459.2 7.0 collective-permute-start.5
  477.2 5.1 collective-permute-start.3
  490.5 10.8 %fusion.67 = f32[2,32,64,128]{3,1,0,2:T(8,128)S(1)} fusion(f32[2,32,64,128]{3,1,0,2:T(8,128)S(1)} %get-tuple-element.276, f32[2,31,64,128]{3,1,0,2:T(8,128)} %get-tuple-element.241, f32[2,1,64,128]{3,1,0,2:T(1,128)S(1)} %get-tuple-element.242, f32[2,1,64,128]{3,1,0,2:T(1,128)S(1)} %get-tuple-element.243, f32[2,31,64,128]{3,1,0,2:T(8,128)} %get-tuple-element.244, ...), kind=kLoop, calls=%fused_computation.8.clone.1 | loop fusion | flops 15728640 | bytes 24347072 | tf_op jit(solution)/shard_map/while/body/eval_jaxpr/mul | solution.py:70
  515.2 7.0 collective-permute-start.5
  533.1 5.1 collective-permute-start.3
  546.5 10.8 %fusion.67 = f32[2,32,64,128]{3,1,0,2:T(8,128)S(1)} fusion(f32[2,32,64,128]{3,1,0,2:T(8,128)S(1)} %get-tuple-element.276, f32[2,31,64,128]{3,1,0,2:T(8,128)} %get-tuple-element.241, f32[2,1,64,128]{3,1,0,2:T(1,128)S(1)} %get-tuple-element.242, f32[2,1,64,128]{3,1,0,2:T(1,128)S(1)} %get-tuple-element.243, f32[2,31,64,128]{3,1,0,2:T(8,128)} %get-tuple-element.244, ...), kind=kLoop, calls=%fused_computation.8.clone.1 | loop fusion | flops 15728640 | bytes 24347072 | tf_op jit(solution)/shard_map/while/body/eval_jaxpr/mul | solution.py:70
  571.2 7.0 collective-permute-start.5
  589.1 5.1 collective-permute-start.3
  602.5 10.8 %fusion.67 = f32[2,32,64,128]{3,1,0,2:T(8,128)S(1)} fusion(f32[2,32,64,128]{3,1,0,2:T(8,128)S(1)} %get-tuple-element.276, f32[2,31,64,128]{3,1,0,2:T(8,128)} %get-tuple-element.241, f32[2,1,64,128]{3,1,0,2:T(1,128)S(1)} %get-tuple-element.242, f32[2,1,64,128]{3,1,0,2:T(1,128)S(1)} %get-tuple-element.243, f32[2,31,64,128]{3,1,0,2:T(8,128)} %get-tuple-element.244, ...), kind=kLoop, calls=%fused_computation.8.clone.1 | loop fusion | flops 15728640 | bytes 24347072 | tf_op jit(solution)/shard_map/while/body/eval_jaxpr/mul | solution.py:70
  627.1 7.0 collective-permute-start.5
  645.1 5.1 collective-permute-start.3
  658.4 10.8 %fusion.67 = f32[2,32,64,128]{3,1,0,2:T(8,128)S(1)} fusion(f32[2,32,64,128]{3,1,0,2:T(8,128)S(1)} %get-tuple-element.276, f32[2,31,64,128]{3,1,0,2:T(8,128)} %get-tuple-element.241, f32[2,1,64,128]{3,1,0,2:T(1,128)S(1)} %get-tuple-element.242, f32[2,1,64,128]{3,1,0,2:T(1,128)S(1)} %get-tuple-element.243, f32[2,31,64,128]{3,1,0,2:T(8,128)} %get-tuple-element.244, ...), kind=kLoop, calls=%fused_computation.8.clone.1 | loop fusion | flops 15728640 | bytes 24347072 | tf_op jit(solution)/shard_map/while/body/eval_jaxpr/mul | solution.py:70
  683.1 7.0 collective-permute-start.5
  701.1 5.1 collective-permute-start.3
  714.4 10.8 %fusion.67 = f32[2,32,64,128]{3,1,0,2:T(8,128)S(1)} fusion(f32[2,32,64,128]{3,1,0,2:T(8,128)S(1)} %get-tuple-element.276, f32[2,31,64,128]{3,1,0,2:T(8,128)} %get-tuple-element.241, f32[2,1,64,128]{3,1,0,2:T(1,128)S(1)} %get-tuple-element.242, f32[2,1,64,128]{3,1,0,2:T(1,128)S(1)} %get-tuple-element.243, f32[2,31,64,128]{3,1,0,2:T(8,128)} %get-tuple-element.244, ...), kind=kLoop, calls=%fused_computation.8.clone.1 | loop fusion | flops 15728640 | bytes 24347072 | tf_op jit(solution)/shard_map/while/body/eval_jaxpr/mul | solution.py:70
  739.1 7.0 collective-permute-start.5
  757.0 5.1 collective-permute-start.3
  770.4 10.8 %fusion.67 = f32[2,32,64,128]{3,1,0,2:T(8,128)S(1)} fusion(f32[2,32,64,128]{3,1,0,2:T(8,128)S(1)} %get-tuple-element.276, f32[2,31,64,128]{3,1,0,2:T(8,128)} %get-tuple-element.241, f32[2,1,64,128]{3,1,0,2:T(1,128)S(1)} %get-tuple-element.242, f32[2,1,64,128]{3,1,0,2:T(1,128)S(1)} %get-tuple-element.243, f32[2,31,64,128]{3,1,0,2:T(8,128)} %get-tuple-element.244, ...), kind=kLoop, calls=%fused_computation.8.clone.1 | loop fusion | flops 15728640 | bytes 24347072 | tf_op jit(solution)/shard_map/while/body/eval_jaxpr/mul | solution.py:70
  795.0 7.0 collective-permute-start.5
  826.4 10.8 %fusion.67 = f32[2,32,64,128]{3,1,0,2:T(8,128)S(1)} fusion(f32[2,32,64,128]{3,1,0,2:T(8,128)S(1)} %get-tuple-element.276, f32[2,31,64,128]{3,1,0,2:T(8,128)} %get-tuple-element.241, f32[2,1,64,128]{3,1,0,2:T(1,128)S(1)} %get-tuple-element.242, f32[2,1,64,128]{3,1,0,2:T(1,128)S(1)} %get-tuple-element.243, f32[2,31,64,128]{3,1,0,2:T(8,128)} %get-tuple-element.244, ...), kind=kLoop, calls=%fused_computation.8.clone.1 | loop fusion | flops 15728640 | bytes 24347072 | tf_op jit(solution)/shard_map/while/body/eval_jaxpr/mul | solution.py:70
  851.0 7.0 collective-permute-start.5
  882.3 10.8 %fusion.67 = f32[2,32,64,128]{3,1,0,2:T(8,128)S(1)} fusion(f32[2,32,64,128]{3,1,0,2:T(8,128)S(1)} %get-tuple-element.276, f32[2,31,64,128]{3,1,0,2:T(8,128)} %get-tuple-element.241, f32[2,1,64,128]{3,1,0,2:T(1,128)S(1)} %get-tuple-element.242, f32[2,1,64,128]{3,1,0,2:T(1,128)S(1)} %get-tuple-element.243, f32[2,31,64,128]{3,1,0,2:T(8,128)} %get-tuple-element.244, ...), kind=kLoop, calls=%fused_computation.8.clone.1 | loop fusion | flops 15728640 | bytes 24347072 | tf_op jit(solution)/shard_map/while/body/eval_jaxpr/mul | solution.py:70
  907.0 7.0 collective-permute-start.5
  938.3 10.8 %fusion.67 = f32[2,32,64,128]{3,1,0,2:T(8,128)S(1)} fusion(f32[2,32,64,128]{3,1,0,2:T(8,128)S(1)} %get-tuple-element.276, f32[2,31,64,128]{3,1,0,2:T(8,128)} %get-tuple-element.241, f32[2,1,64,128]{3,1,0,2:T(1,128)S(1)} %get-tuple-element.242, f32[2,1,64,128]{3,1,0,2:T(1,128)S(1)} %get-tuple-element.243, f32[2,31,64,128]{3,1,0,2:T(8,128)} %get-tuple-element.244, ...), kind=kLoop, calls=%fused_computation.8.clone.1 | loop fusion | flops 15728640 | bytes 24347072 | tf_op jit(solution)/shard_map/while/body/eval_jaxpr/mul | solution.py:70
  (568 shorter events, 587.2 us)
Async XLA Ops:
  3.6 42.3 %collective-permute-start.9 = (f32[2,32,1,128]{3,1,0,2:T(8,128)S(1)}, f32[2,32,1,128]{3,1,0,2:T(8,128)}, u32[]{:S(2)}, u32[]{:S(2)}) collective-permute-start(f32[2,32,1,128]{3,1,0,2:T(8,128)S(1)} %get-tuple-element.144), channel_id=1, source_target_pairs={{4,0},{8,4},{12,8},{5,1},{9,5},{13,9},{6,2},{10,6},{14,10},{7,3},{... | collective-permute-start | bytes 98312 | tf_op jit(solution)/shard_map/ppermute | solution.py:12
  4.9 41.9 %collective-permute-start.8 = (f32[2,32,1,128]{3,1,0,2:T(8,128)S(1)}, f32[2,32,1,128]{3,1,0,2:T(8,128)}, u32[]{:S(2)}, u32[]{:S(2)}) collective-permute-start(f32[2,32,1,128]{3,1,0,2:T(8,128)S(1)} %get-tuple-element.145), channel_id=1, source_target_pairs={{0,4},{4,8},{8,12},{1,5},{5,9},{9,13},{2,6},{6,10},{10,14},{3,7},{... | collective-permute-start | bytes 98312 | tf_op jit(solution)/shard_map/ppermute | solution.py:12
  59.8 37.9 %collective-permute-start.1 = (f32[2,32,64,1]{2,1,0,3:T(8,128)S(1)}, f32[2,32,64,1]{2,1,0,3:T(8,128)}, u32[]{:S(2)}, u32[]{:S(2)}) collective-permute-start(f32[2,32,64,1]{2,1,0,3:T(8,128)S(1)} %get-tuple-element.250), channel_id=1, source_target_pairs={{0,1},{1,2},{2,3},{4,5},{5,6},{6,7},{8,9},{9,10},{10,11},{12,13},{... | collective-permute-start | bytes 49160 | tf_op jit(solution)/shard_map/while/body/eval_jaxpr/ppermute | solution.py:12
  65.7 32.9 %collective-permute-start.4 = (f32[2,1,64,128]{3,1,0,2:T(1,128)S(1)}, f32[2,1,64,128]{3,1,0,2:T(1,128)S(1)}, u32[]{:S(2)}, u32[]{:S(2)}) collective-permute-start(f32[2,1,64,128]{3,1,0,2:T(1,128)S(1)} %get-tuple-element.243), channel_id=1, source_target_pairs={{16,0},{32,16},{48,32},{64,48},{80,64},{96,80},{112,96},{17,1},{33... | collective-permute-start | bytes 196616 | tf_op jit(solution)/shard_map/while/body/eval_jaxpr/ppermute | solution.py:12
  67.0 31.6 %collective-permute-start.5 = (f32[2,1,64,128]{3,1,0,2:T(1,128)S(1)}, f32[2,1,64,128]{3,1,0,2:T(1,128)}, u32[]{:S(2)}, u32[]{:S(2)}) collective-permute-start(f32[2,1,64,128]{3,1,0,2:T(1,128)S(1)} %get-tuple-element.242), channel_id=1, source_target_pairs={{0,16},{16,32},{32,48},{48,64},{64,80},{80,96},{96,112},{1,17},{17... | collective-permute-start | bytes 196616 | tf_op jit(solution)/shard_map/while/body/eval_jaxpr/ppermute | solution.py:12
  118.3 35.5 %collective-permute-start.1 = (f32[2,32,64,1]{2,1,0,3:T(8,128)S(1)}, f32[2,32,64,1]{2,1,0,3:T(8,128)}, u32[]{:S(2)}, u32[]{:S(2)}) collective-permute-start(f32[2,32,64,1]{2,1,0,3:T(8,128)S(1)} %get-tuple-element.250), channel_id=1, source_target_pairs={{0,1},{1,2},{2,3},{4,5},{5,6},{6,7},{8,9},{9,10},{10,11},{12,13},{... | collective-permute-start | bytes 49160 | tf_op jit(solution)/shard_map/while/body/eval_jaxpr/ppermute | solution.py:12
  122.4 32.3 %collective-permute-start.4 = (f32[2,1,64,128]{3,1,0,2:T(1,128)S(1)}, f32[2,1,64,128]{3,1,0,2:T(1,128)S(1)}, u32[]{:S(2)}, u32[]{:S(2)}) collective-permute-start(f32[2,1,64,128]{3,1,0,2:T(1,128)S(1)} %get-tuple-element.243), channel_id=1, source_target_pairs={{16,0},{32,16},{48,32},{64,48},{80,64},{96,80},{112,96},{17,1},{33... | collective-permute-start | bytes 196616 | tf_op jit(solution)/shard_map/while/body/eval_jaxpr/ppermute | solution.py:12
  174.3 35.4 %collective-permute-start.1 = (f32[2,32,64,1]{2,1,0,3:T(8,128)S(1)}, f32[2,32,64,1]{2,1,0,3:T(8,128)}, u32[]{:S(2)}, u32[]{:S(2)}) collective-permute-start(f32[2,32,64,1]{2,1,0,3:T(8,128)S(1)} %get-tuple-element.250), channel_id=1, source_target_pairs={{0,1},{1,2},{2,3},{4,5},{5,6},{6,7},{8,9},{9,10},{10,11},{12,13},{... | collective-permute-start | bytes 49160 | tf_op jit(solution)/shard_map/while/body/eval_jaxpr/ppermute | solution.py:12
  178.1 32.6 %collective-permute-start.4 = (f32[2,1,64,128]{3,1,0,2:T(1,128)S(1)}, f32[2,1,64,128]{3,1,0,2:T(1,128)S(1)}, u32[]{:S(2)}, u32[]{:S(2)}) collective-permute-start(f32[2,1,64,128]{3,1,0,2:T(1,128)S(1)} %get-tuple-element.243), channel_id=1, source_target_pairs={{16,0},{32,16},{48,32},{64,48},{80,64},{96,80},{112,96},{17,1},{33... | collective-permute-start | bytes 196616 | tf_op jit(solution)/shard_map/while/body/eval_jaxpr/ppermute | solution.py:12
  179.4 31.3 %collective-permute-start.5 = (f32[2,1,64,128]{3,1,0,2:T(1,128)S(1)}, f32[2,1,64,128]{3,1,0,2:T(1,128)}, u32[]{:S(2)}, u32[]{:S(2)}) collective-permute-start(f32[2,1,64,128]{3,1,0,2:T(1,128)S(1)} %get-tuple-element.242), channel_id=1, source_target_pairs={{0,16},{16,32},{32,48},{48,64},{64,80},{80,96},{96,112},{1,17},{17... | collective-permute-start | bytes 196616 | tf_op jit(solution)/shard_map/while/body/eval_jaxpr/ppermute | solution.py:12
  230.3 35.4 %collective-permute-start.1 = (f32[2,32,64,1]{2,1,0,3:T(8,128)S(1)}, f32[2,32,64,1]{2,1,0,3:T(8,128)}, u32[]{:S(2)}, u32[]{:S(2)}) collective-permute-start(f32[2,32,64,1]{2,1,0,3:T(8,128)S(1)} %get-tuple-element.250), channel_id=1, source_target_pairs={{0,1},{1,2},{2,3},{4,5},{5,6},{6,7},{8,9},{9,10},{10,11},{12,13},{... | collective-permute-start | bytes 49160 | tf_op jit(solution)/shard_map/while/body/eval_jaxpr/ppermute | solution.py:12
  234.0 32.6 %collective-permute-start.4 = (f32[2,1,64,128]{3,1,0,2:T(1,128)S(1)}, f32[2,1,64,128]{3,1,0,2:T(1,128)S(1)}, u32[]{:S(2)}, u32[]{:S(2)}) collective-permute-start(f32[2,1,64,128]{3,1,0,2:T(1,128)S(1)} %get-tuple-element.243), channel_id=1, source_target_pairs={{16,0},{32,16},{48,32},{64,48},{80,64},{96,80},{112,96},{17,1},{33... | collective-permute-start | bytes 196616 | tf_op jit(solution)/shard_map/while/body/eval_jaxpr/ppermute | solution.py:12
  235.3 31.3 %collective-permute-start.5 = (f32[2,1,64,128]{3,1,0,2:T(1,128)S(1)}, f32[2,1,64,128]{3,1,0,2:T(1,128)}, u32[]{:S(2)}, u32[]{:S(2)}) collective-permute-start(f32[2,1,64,128]{3,1,0,2:T(1,128)S(1)} %get-tuple-element.242), channel_id=1, source_target_pairs={{0,16},{16,32},{32,48},{48,64},{64,80},{80,96},{96,112},{1,17},{17... | collective-permute-start | bytes 196616 | tf_op jit(solution)/shard_map/while/body/eval_jaxpr/ppermute | solution.py:12
  286.3 35.4 %collective-permute-start.1 = (f32[2,32,64,1]{2,1,0,3:T(8,128)S(1)}, f32[2,32,64,1]{2,1,0,3:T(8,128)}, u32[]{:S(2)}, u32[]{:S(2)}) collective-permute-start(f32[2,32,64,1]{2,1,0,3:T(8,128)S(1)} %get-tuple-element.250), channel_id=1, source_target_pairs={{0,1},{1,2},{2,3},{4,5},{5,6},{6,7},{8,9},{9,10},{10,11},{12,13},{... | collective-permute-start | bytes 49160 | tf_op jit(solution)/shard_map/while/body/eval_jaxpr/ppermute | solution.py:12
  290.0 32.6 %collective-permute-start.4 = (f32[2,1,64,128]{3,1,0,2:T(1,128)S(1)}, f32[2,1,64,128]{3,1,0,2:T(1,128)S(1)}, u32[]{:S(2)}, u32[]{:S(2)}) collective-permute-start(f32[2,1,64,128]{3,1,0,2:T(1,128)S(1)} %get-tuple-element.243), channel_id=1, source_target_pairs={{16,0},{32,16},{48,32},{64,48},{80,64},{96,80},{112,96},{17,1},{33... | collective-permute-start | bytes 196616 | tf_op jit(solution)/shard_map/while/body/eval_jaxpr/ppermute | solution.py:12
  291.3 31.3 %collective-permute-start.5 = (f32[2,1,64,128]{3,1,0,2:T(1,128)S(1)}, f32[2,1,64,128]{3,1,0,2:T(1,128)}, u32[]{:S(2)}, u32[]{:S(2)}) collective-permute-start(f32[2,1,64,128]{3,1,0,2:T(1,128)S(1)} %get-tuple-element.242), channel_id=1, source_target_pairs={{0,16},{16,32},{32,48},{48,64},{64,80},{80,96},{96,112},{1,17},{17... | collective-permute-start | bytes 196616 | tf_op jit(solution)/shard_map/while/body/eval_jaxpr/ppermute | solution.py:12
  342.3 35.4 %collective-permute-start.1 = (f32[2,32,64,1]{2,1,0,3:T(8,128)S(1)}, f32[2,32,64,1]{2,1,0,3:T(8,128)}, u32[]{:S(2)}, u32[]{:S(2)}) collective-permute-start(f32[2,32,64,1]{2,1,0,3:T(8,128)S(1)} %get-tuple-element.250), channel_id=1, source_target_pairs={{0,1},{1,2},{2,3},{4,5},{5,6},{6,7},{8,9},{9,10},{10,11},{12,13},{... | collective-permute-start | bytes 49160 | tf_op jit(solution)/shard_map/while/body/eval_jaxpr/ppermute | solution.py:12
  346.0 32.6 %collective-permute-start.4 = (f32[2,1,64,128]{3,1,0,2:T(1,128)S(1)}, f32[2,1,64,128]{3,1,0,2:T(1,128)S(1)}, u32[]{:S(2)}, u32[]{:S(2)}) collective-permute-start(f32[2,1,64,128]{3,1,0,2:T(1,128)S(1)} %get-tuple-element.243), channel_id=1, source_target_pairs={{16,0},{32,16},{48,32},{64,48},{80,64},{96,80},{112,96},{17,1},{33... | collective-permute-start | bytes 196616 | tf_op jit(solution)/shard_map/while/body/eval_jaxpr/ppermute | solution.py:12
  347.3 31.3 %collective-permute-start.5 = (f32[2,1,64,128]{3,1,0,2:T(1,128)S(1)}, f32[2,1,64,128]{3,1,0,2:T(1,128)}, u32[]{:S(2)}, u32[]{:S(2)}) collective-permute-start(f32[2,1,64,128]{3,1,0,2:T(1,128)S(1)} %get-tuple-element.242), channel_id=1, source_target_pairs={{0,16},{16,32},{32,48},{48,64},{64,80},{80,96},{96,112},{1,17},{17... | collective-permute-start | bytes 196616 | tf_op jit(solution)/shard_map/while/body/eval_jaxpr/ppermute | solution.py:12
  398.2 35.4 %collective-permute-start.1 = (f32[2,32,64,1]{2,1,0,3:T(8,128)S(1)}, f32[2,32,64,1]{2,1,0,3:T(8,128)}, u32[]{:S(2)}, u32[]{:S(2)}) collective-permute-start(f32[2,32,64,1]{2,1,0,3:T(8,128)S(1)} %get-tuple-element.250), channel_id=1, source_target_pairs={{0,1},{1,2},{2,3},{4,5},{5,6},{6,7},{8,9},{9,10},{10,11},{12,13},{... | collective-permute-start | bytes 49160 | tf_op jit(solution)/shard_map/while/body/eval_jaxpr/ppermute | solution.py:12
  402.0 32.6 %collective-permute-start.4 = (f32[2,1,64,128]{3,1,0,2:T(1,128)S(1)}, f32[2,1,64,128]{3,1,0,2:T(1,128)S(1)}, u32[]{:S(2)}, u32[]{:S(2)}) collective-permute-start(f32[2,1,64,128]{3,1,0,2:T(1,128)S(1)} %get-tuple-element.243), channel_id=1, source_target_pairs={{16,0},{32,16},{48,32},{64,48},{80,64},{96,80},{112,96},{17,1},{33... | collective-permute-start | bytes 196616 | tf_op jit(solution)/shard_map/while/body/eval_jaxpr/ppermute | solution.py:12
  403.3 31.3 %collective-permute-start.5 = (f32[2,1,64,128]{3,1,0,2:T(1,128)S(1)}, f32[2,1,64,128]{3,1,0,2:T(1,128)}, u32[]{:S(2)}, u32[]{:S(2)}) collective-permute-start(f32[2,1,64,128]{3,1,0,2:T(1,128)S(1)} %get-tuple-element.242), channel_id=1, source_target_pairs={{0,16},{16,32},{32,48},{48,64},{64,80},{80,96},{96,112},{1,17},{17... | collective-permute-start | bytes 196616 | tf_op jit(solution)/shard_map/while/body/eval_jaxpr/ppermute | solution.py:12
  454.2 35.4 %collective-permute-start.1 = (f32[2,32,64,1]{2,1,0,3:T(8,128)S(1)}, f32[2,32,64,1]{2,1,0,3:T(8,128)}, u32[]{:S(2)}, u32[]{:S(2)}) collective-permute-start(f32[2,32,64,1]{2,1,0,3:T(8,128)S(1)} %get-tuple-element.250), channel_id=1, source_target_pairs={{0,1},{1,2},{2,3},{4,5},{5,6},{6,7},{8,9},{9,10},{10,11},{12,13},{... | collective-permute-start | bytes 49160 | tf_op jit(solution)/shard_map/while/body/eval_jaxpr/ppermute | solution.py:12
  457.9 32.6 %collective-permute-start.4 = (f32[2,1,64,128]{3,1,0,2:T(1,128)S(1)}, f32[2,1,64,128]{3,1,0,2:T(1,128)S(1)}, u32[]{:S(2)}, u32[]{:S(2)}) collective-permute-start(f32[2,1,64,128]{3,1,0,2:T(1,128)S(1)} %get-tuple-element.243), channel_id=1, source_target_pairs={{16,0},{32,16},{48,32},{64,48},{80,64},{96,80},{112,96},{17,1},{33... | collective-permute-start | bytes 196616 | tf_op jit(solution)/shard_map/while/body/eval_jaxpr/ppermute | solution.py:12
  459.2 31.3 %collective-permute-start.5 = (f32[2,1,64,128]{3,1,0,2:T(1,128)S(1)}, f32[2,1,64,128]{3,1,0,2:T(1,128)}, u32[]{:S(2)}, u32[]{:S(2)}) collective-permute-start(f32[2,1,64,128]{3,1,0,2:T(1,128)S(1)} %get-tuple-element.242), channel_id=1, source_target_pairs={{0,16},{16,32},{32,48},{48,64},{64,80},{80,96},{96,112},{1,17},{17... | collective-permute-start | bytes 196616 | tf_op jit(solution)/shard_map/while/body/eval_jaxpr/ppermute | solution.py:12
  510.2 35.4 %collective-permute-start.1 = (f32[2,32,64,1]{2,1,0,3:T(8,128)S(1)}, f32[2,32,64,1]{2,1,0,3:T(8,128)}, u32[]{:S(2)}, u32[]{:S(2)}) collective-permute-start(f32[2,32,64,1]{2,1,0,3:T(8,128)S(1)} %get-tuple-element.250), channel_id=1, source_target_pairs={{0,1},{1,2},{2,3},{4,5},{5,6},{6,7},{8,9},{9,10},{10,11},{12,13},{... | collective-permute-start | bytes 49160 | tf_op jit(solution)/shard_map/while/body/eval_jaxpr/ppermute | solution.py:12
  513.9 32.6 %collective-permute-start.4 = (f32[2,1,64,128]{3,1,0,2:T(1,128)S(1)}, f32[2,1,64,128]{3,1,0,2:T(1,128)S(1)}, u32[]{:S(2)}, u32[]{:S(2)}) collective-permute-start(f32[2,1,64,128]{3,1,0,2:T(1,128)S(1)} %get-tuple-element.243), channel_id=1, source_target_pairs={{16,0},{32,16},{48,32},{64,48},{80,64},{96,80},{112,96},{17,1},{33... | collective-permute-start | bytes 196616 | tf_op jit(solution)/shard_map/while/body/eval_jaxpr/ppermute | solution.py:12
  515.2 31.3 %collective-permute-start.5 = (f32[2,1,64,128]{3,1,0,2:T(1,128)S(1)}, f32[2,1,64,128]{3,1,0,2:T(1,128)}, u32[]{:S(2)}, u32[]{:S(2)}) collective-permute-start(f32[2,1,64,128]{3,1,0,2:T(1,128)S(1)} %get-tuple-element.242), channel_id=1, source_target_pairs={{0,16},{16,32},{32,48},{48,64},{64,80},{80,96},{96,112},{1,17},{17... | collective-permute-start | bytes 196616 | tf_op jit(solution)/shard_map/while/body/eval_jaxpr/ppermute | solution.py:12
  566.1 35.4 %collective-permute-start.1 = (f32[2,32,64,1]{2,1,0,3:T(8,128)S(1)}, f32[2,32,64,1]{2,1,0,3:T(8,128)}, u32[]{:S(2)}, u32[]{:S(2)}) collective-permute-start(f32[2,32,64,1]{2,1,0,3:T(8,128)S(1)} %get-tuple-element.250), channel_id=1, source_target_pairs={{0,1},{1,2},{2,3},{4,5},{5,6},{6,7},{8,9},{9,10},{10,11},{12,13},{... | collective-permute-start | bytes 49160 | tf_op jit(solution)/shard_map/while/body/eval_jaxpr/ppermute | solution.py:12
  569.9 32.6 %collective-permute-start.4 = (f32[2,1,64,128]{3,1,0,2:T(1,128)S(1)}, f32[2,1,64,128]{3,1,0,2:T(1,128)S(1)}, u32[]{:S(2)}, u32[]{:S(2)}) collective-permute-start(f32[2,1,64,128]{3,1,0,2:T(1,128)S(1)} %get-tuple-element.243), channel_id=1, source_target_pairs={{16,0},{32,16},{48,32},{64,48},{80,64},{96,80},{112,96},{17,1},{33... | collective-permute-start | bytes 196616 | tf_op jit(solution)/shard_map/while/body/eval_jaxpr/ppermute | solution.py:12
  571.2 31.3 %collective-permute-start.5 = (f32[2,1,64,128]{3,1,0,2:T(1,128)S(1)}, f32[2,1,64,128]{3,1,0,2:T(1,128)}, u32[]{:S(2)}, u32[]{:S(2)}) collective-permute-start(f32[2,1,64,128]{3,1,0,2:T(1,128)S(1)} %get-tuple-element.242), channel_id=1, source_target_pairs={{0,16},{16,32},{32,48},{48,64},{64,80},{80,96},{96,112},{1,17},{17... | collective-permute-start | bytes 196616 | tf_op jit(solution)/shard_map/while/body/eval_jaxpr/ppermute | solution.py:12
  622.1 35.4 %collective-permute-start.1 = (f32[2,32,64,1]{2,1,0,3:T(8,128)S(1)}, f32[2,32,64,1]{2,1,0,3:T(8,128)}, u32[]{:S(2)}, u32[]{:S(2)}) collective-permute-start(f32[2,32,64,1]{2,1,0,3:T(8,128)S(1)} %get-tuple-element.250), channel_id=1, source_target_pairs={{0,1},{1,2},{2,3},{4,5},{5,6},{6,7},{8,9},{9,10},{10,11},{12,13},{... | collective-permute-start | bytes 49160 | tf_op jit(solution)/shard_map/while/body/eval_jaxpr/ppermute | solution.py:12
  625.8 32.6 %collective-permute-start.4 = (f32[2,1,64,128]{3,1,0,2:T(1,128)S(1)}, f32[2,1,64,128]{3,1,0,2:T(1,128)S(1)}, u32[]{:S(2)}, u32[]{:S(2)}) collective-permute-start(f32[2,1,64,128]{3,1,0,2:T(1,128)S(1)} %get-tuple-element.243), channel_id=1, source_target_pairs={{16,0},{32,16},{48,32},{64,48},{80,64},{96,80},{112,96},{17,1},{33... | collective-permute-start | bytes 196616 | tf_op jit(solution)/shard_map/while/body/eval_jaxpr/ppermute | solution.py:12
  627.1 31.3 %collective-permute-start.5 = (f32[2,1,64,128]{3,1,0,2:T(1,128)S(1)}, f32[2,1,64,128]{3,1,0,2:T(1,128)}, u32[]{:S(2)}, u32[]{:S(2)}) collective-permute-start(f32[2,1,64,128]{3,1,0,2:T(1,128)S(1)} %get-tuple-element.242), channel_id=1, source_target_pairs={{0,16},{16,32},{32,48},{48,64},{64,80},{80,96},{96,112},{1,17},{17... | collective-permute-start | bytes 196616 | tf_op jit(solution)/shard_map/while/body/eval_jaxpr/ppermute | solution.py:12
  678.1 35.4 %collective-permute-start.1 = (f32[2,32,64,1]{2,1,0,3:T(8,128)S(1)}, f32[2,32,64,1]{2,1,0,3:T(8,128)}, u32[]{:S(2)}, u32[]{:S(2)}) collective-permute-start(f32[2,32,64,1]{2,1,0,3:T(8,128)S(1)} %get-tuple-element.250), channel_id=1, source_target_pairs={{0,1},{1,2},{2,3},{4,5},{5,6},{6,7},{8,9},{9,10},{10,11},{12,13},{... | collective-permute-start | bytes 49160 | tf_op jit(solution)/shard_map/while/body/eval_jaxpr/ppermute | solution.py:12
  681.8 32.6 %collective-permute-start.4 = (f32[2,1,64,128]{3,1,0,2:T(1,128)S(1)}, f32[2,1,64,128]{3,1,0,2:T(1,128)S(1)}, u32[]{:S(2)}, u32[]{:S(2)}) collective-permute-start(f32[2,1,64,128]{3,1,0,2:T(1,128)S(1)} %get-tuple-element.243), channel_id=1, source_target_pairs={{16,0},{32,16},{48,32},{64,48},{80,64},{96,80},{112,96},{17,1},{33... | collective-permute-start | bytes 196616 | tf_op jit(solution)/shard_map/while/body/eval_jaxpr/ppermute | solution.py:12
  683.1 31.3 %collective-permute-start.5 = (f32[2,1,64,128]{3,1,0,2:T(1,128)S(1)}, f32[2,1,64,128]{3,1,0,2:T(1,128)}, u32[]{:S(2)}, u32[]{:S(2)}) collective-permute-start(f32[2,1,64,128]{3,1,0,2:T(1,128)S(1)} %get-tuple-element.242), channel_id=1, source_target_pairs={{0,16},{16,32},{32,48},{48,64},{64,80},{80,96},{96,112},{1,17},{17... | collective-permute-start | bytes 196616 | tf_op jit(solution)/shard_map/while/body/eval_jaxpr/ppermute | solution.py:12
  734.0 35.4 %collective-permute-start.1 = (f32[2,32,64,1]{2,1,0,3:T(8,128)S(1)}, f32[2,32,64,1]{2,1,0,3:T(8,128)}, u32[]{:S(2)}, u32[]{:S(2)}) collective-permute-start(f32[2,32,64,1]{2,1,0,3:T(8,128)S(1)} %get-tuple-element.250), channel_id=1, source_target_pairs={{0,1},{1,2},{2,3},{4,5},{5,6},{6,7},{8,9},{9,10},{10,11},{12,13},{... | collective-permute-start | bytes 49160 | tf_op jit(solution)/shard_map/while/body/eval_jaxpr/ppermute | solution.py:12
  737.8 32.6 %collective-permute-start.4 = (f32[2,1,64,128]{3,1,0,2:T(1,128)S(1)}, f32[2,1,64,128]{3,1,0,2:T(1,128)S(1)}, u32[]{:S(2)}, u32[]{:S(2)}) collective-permute-start(f32[2,1,64,128]{3,1,0,2:T(1,128)S(1)} %get-tuple-element.243), channel_id=1, source_target_pairs={{16,0},{32,16},{48,32},{64,48},{80,64},{96,80},{112,96},{17,1},{33... | collective-permute-start | bytes 196616 | tf_op jit(solution)/shard_map/while/body/eval_jaxpr/ppermute | solution.py:12
  739.1 31.3 %collective-permute-start.5 = (f32[2,1,64,128]{3,1,0,2:T(1,128)S(1)}, f32[2,1,64,128]{3,1,0,2:T(1,128)}, u32[]{:S(2)}, u32[]{:S(2)}) collective-permute-start(f32[2,1,64,128]{3,1,0,2:T(1,128)S(1)} %get-tuple-element.242), channel_id=1, source_target_pairs={{0,16},{16,32},{32,48},{48,64},{64,80},{80,96},{96,112},{1,17},{17... | collective-permute-start | bytes 196616 | tf_op jit(solution)/shard_map/while/body/eval_jaxpr/ppermute | solution.py:12
  790.0 35.4 %collective-permute-start.1 = (f32[2,32,64,1]{2,1,0,3:T(8,128)S(1)}, f32[2,32,64,1]{2,1,0,3:T(8,128)}, u32[]{:S(2)}, u32[]{:S(2)}) collective-permute-start(f32[2,32,64,1]{2,1,0,3:T(8,128)S(1)} %get-tuple-element.250), channel_id=1, source_target_pairs={{0,1},{1,2},{2,3},{4,5},{5,6},{6,7},{8,9},{9,10},{10,11},{12,13},{... | collective-permute-start | bytes 49160 | tf_op jit(solution)/shard_map/while/body/eval_jaxpr/ppermute | solution.py:12
  793.7 32.6 %collective-permute-start.4 = (f32[2,1,64,128]{3,1,0,2:T(1,128)S(1)}, f32[2,1,64,128]{3,1,0,2:T(1,128)S(1)}, u32[]{:S(2)}, u32[]{:S(2)}) collective-permute-start(f32[2,1,64,128]{3,1,0,2:T(1,128)S(1)} %get-tuple-element.243), channel_id=1, source_target_pairs={{16,0},{32,16},{48,32},{64,48},{80,64},{96,80},{112,96},{17,1},{33... | collective-permute-start | bytes 196616 | tf_op jit(solution)/shard_map/while/body/eval_jaxpr/ppermute | solution.py:12
  795.0 31.3 %collective-permute-start.5 = (f32[2,1,64,128]{3,1,0,2:T(1,128)S(1)}, f32[2,1,64,128]{3,1,0,2:T(1,128)}, u32[]{:S(2)}, u32[]{:S(2)}) collective-permute-start(f32[2,1,64,128]{3,1,0,2:T(1,128)S(1)} %get-tuple-element.242), channel_id=1, source_target_pairs={{0,16},{16,32},{32,48},{48,64},{64,80},{80,96},{96,112},{1,17},{17... | collective-permute-start | bytes 196616 | tf_op jit(solution)/shard_map/while/body/eval_jaxpr/ppermute | solution.py:12
  846.0 35.4 %collective-permute-start.1 = (f32[2,32,64,1]{2,1,0,3:T(8,128)S(1)}, f32[2,32,64,1]{2,1,0,3:T(8,128)}, u32[]{:S(2)}, u32[]{:S(2)}) collective-permute-start(f32[2,32,64,1]{2,1,0,3:T(8,128)S(1)} %get-tuple-element.250), channel_id=1, source_target_pairs={{0,1},{1,2},{2,3},{4,5},{5,6},{6,7},{8,9},{9,10},{10,11},{12,13},{... | collective-permute-start | bytes 49160 | tf_op jit(solution)/shard_map/while/body/eval_jaxpr/ppermute | solution.py:12
  849.7 32.6 %collective-permute-start.4 = (f32[2,1,64,128]{3,1,0,2:T(1,128)S(1)}, f32[2,1,64,128]{3,1,0,2:T(1,128)S(1)}, u32[]{:S(2)}, u32[]{:S(2)}) collective-permute-start(f32[2,1,64,128]{3,1,0,2:T(1,128)S(1)} %get-tuple-element.243), channel_id=1, source_target_pairs={{16,0},{32,16},{48,32},{64,48},{80,64},{96,80},{112,96},{17,1},{33... | collective-permute-start | bytes 196616 | tf_op jit(solution)/shard_map/while/body/eval_jaxpr/ppermute | solution.py:12
  851.0 31.3 %collective-permute-start.5 = (f32[2,1,64,128]{3,1,0,2:T(1,128)S(1)}, f32[2,1,64,128]{3,1,0,2:T(1,128)}, u32[]{:S(2)}, u32[]{:S(2)}) collective-permute-start(f32[2,1,64,128]{3,1,0,2:T(1,128)S(1)} %get-tuple-element.242), channel_id=1, source_target_pairs={{0,16},{16,32},{32,48},{48,64},{64,80},{80,96},{96,112},{1,17},{17... | collective-permute-start | bytes 196616 | tf_op jit(solution)/shard_map/while/body/eval_jaxpr/ppermute | solution.py:12
  902.0 35.4 %collective-permute-start.1 = (f32[2,32,64,1]{2,1,0,3:T(8,128)S(1)}, f32[2,32,64,1]{2,1,0,3:T(8,128)}, u32[]{:S(2)}, u32[]{:S(2)}) collective-permute-start(f32[2,32,64,1]{2,1,0,3:T(8,128)S(1)} %get-tuple-element.250), channel_id=1, source_target_pairs={{0,1},{1,2},{2,3},{4,5},{5,6},{6,7},{8,9},{9,10},{10,11},{12,13},{... | collective-permute-start | bytes 49160 | tf_op jit(solution)/shard_map/while/body/eval_jaxpr/ppermute | solution.py:12
  905.7 32.6 %collective-permute-start.4 = (f32[2,1,64,128]{3,1,0,2:T(1,128)S(1)}, f32[2,1,64,128]{3,1,0,2:T(1,128)S(1)}, u32[]{:S(2)}, u32[]{:S(2)}) collective-permute-start(f32[2,1,64,128]{3,1,0,2:T(1,128)S(1)} %get-tuple-element.243), channel_id=1, source_target_pairs={{16,0},{32,16},{48,32},{64,48},{80,64},{96,80},{112,96},{17,1},{33... | collective-permute-start | bytes 196616 | tf_op jit(solution)/shard_map/while/body/eval_jaxpr/ppermute | solution.py:12
  (100 other events, 1545.2 us)
where the time goes:
time: 960 us; the launch traced here: 954 us
  local copies, waits for them, and re-layouts  366 us (38%)
  starting transfers between devices  333 us (35%)
  other arithmetic  252 us (26%)
    ppermute x102, starting transfers between devices, from_behind(): return lax.ppermute(block, axis, route)  333 us
    mul x16, other arithmetic, single_step(): flux = conduct[None] * flux  173 us
    slice x48, local copies, waits for them, and re-layouts, beside(): up = jnp.where(place == count - 1, upper, jnp.roll(fields, -1, axis=dim))  134 us
    another operation x16, local copies, waits for them, and re-layouts  73.4 us
    slice x65, local copies, waits for them, and re-layouts, end_planes(): first = lax.slice_in_dim(fields, 0, 1, axis=dim)  63.1 us
    slice x17, local copies, waits for them, and re-layouts, end_planes(): last = lax.slice_in_dim(fields, count - 1, count, axis=dim)  50.1 us
    sub x16, other arithmetic, single_step(): new_acid = acid + diffusion[0] * flux[0] - reacted  30.4 us
    eq x51, other arithmetic, beside(): up = jnp.where(place == count - 1, upper, jnp.roll(fields, -1, axis=dim))  20.5 us
  transfers between devices with their start and end apart: 102, of which 0 were waited for; matrix products, arithmetic and copies ran while one was open for 33% of the time, Pallas kernels for 0%

commit v1 on v0

v1 whole, which is shorter than its diff:
```python
import functools

import jax
import jax.numpy as jnp
from jax import lax
from jax.experimental import pallas as pl
from jax.experimental.pallas import tpu as pltpu
from jax.sharding import PartitionSpec as P

STEPS = 16
DEEP = 4
NX, NY, NZ = 32, 64, 128
XF = NX + 2 * DEEP
YF = NY + 32
ROW = 16
GROUP, GROUP_DOT, GROUP_STRIPS = 2, 20, 8
TILES = NY // 8 + 2
VMEM = pl.BlockSpec(memory_space=pltpu.VMEM)
SMEM = pl.BlockSpec(memory_space=pltpu.SMEM)
LIMIT = 48 * 1024 * 1024


def lanes():
    return lax.broadcasted_iota(jnp.int32, (8, 128), 1)


def rows():
    return lax.broadcasted_iota(jnp.int32, (8, 128), 0)


def roll(tile, shift, axis=1):
    size = tile.shape[axis]
    shift = shift % size
    return pltpu.roll(tile, shift, axis) if shift else tile


def ring(block, axis, distance):
    size = lax.axis_size(axis)
    return lax.ppermute(block, axis, [(i, (i + distance) % size) for i in range(size)])


def split(block, terms):
    parts = []
    for _ in range(terms):
        part = block.astype(jnp.bfloat16)
        block = block - part.astype(jnp.float32)
        parts.append(part)
    return jnp.concatenate(parts, axis=-1)


def zeros_and_ones(kind, terms):
    i = lax.broadcasted_iota(jnp.int32, (128, 128), 0)
    j = lax.broadcasted_iota(jnp.int32, (128, 128), 1)
    ones = (i == j + 1) | (i + 1 == j) if kind == "near" else i == (j ^ 7)
    return jnp.concatenate([jnp.where(ones, 1.0, 0.0).astype(jnp.bfloat16)] * terms, axis=0)


def pack_strips(edges, right, left, fields, skip):
    low = (lanes() & 7) < 4
    half = NX // 2
    back = zeros_and_ones("turn", 3)
    for f in range(fields):
        turned = jnp.dot(
            split(edges[f, skip : skip + NX].reshape(NX * 8, 128), 3), back, preferred_element_type=jnp.float32
        ).reshape(NX, 8, 128)
        for x in range(half):
            near, far = turned[x], turned[x + half]
            right[f, x] = jnp.where(low, roll(far, -4), near)
            left[f, x] = jnp.where(low, near, roll(far, 4))


def prepare(conc, pore, perm, rate, fields, xlo, xhi, right, left, edges):
    lane = lanes()

    def plane(x):
        strip = [jnp.zeros((8, 128), jnp.float32)] * 4
        for t in range(1, 9):
            here = pl.ds(8 * (t - 1), 8)
            solid = pore[x, here, :].astype(jnp.float32)
            k = solid * perm[x, here, :]
            r = solid * rate[x, here, :]
            for f, value in enumerate((k * conc[0, x, here, :], k * conc[1, x, here, :], k, r)):
                fields[f, x, here, :] = value
                strip[f] = jnp.where((lane >> 3) == t, roll(value, 8 * t + 4), strip[f])
        for f in range(4):
            edges[f, x] = strip[f]

    grouped(0, NX, GROUP, plane)
    for f in range(4):
        xlo[f] = fields[f, 0:DEEP]
        xhi[f] = fields[f, NX - DEEP : NX]
    pack_strips(edges, right, left, 4, 0)


def strips_in(flags, fields, from_left, from_right, strips, ylo, yhi, *, count):
    lane, row = lanes(), rows()
    low = (lane & 7) < 4
    left_ok, right_ok = flags[4], flags[5]
    half = NX // 2
    for f in range(count):

        for x in range(half):
            before, after = from_left[f, x] * left_ok, from_right[f, x] * right_ok
            strips[f, x] = jnp.where(low, after, before)
            strips[f, x + half] = jnp.where(low, roll(after, -4), roll(before, 4))
        for x in range(NX):
            ylo[f, x] = fields[f, x, 0:4, :]
            yhi[f, x] = fields[f, x, NY - 4 : NY, :]
        for group in range(2):
            first = jnp.zeros((8, 128), jnp.float32)
            last = first
            for i in range(16):
                strip = strips[f, group * 16 + i]
                mine = (lane >> 3) == i
                first = jnp.where(mine, roll(strip, 8 * i - 8), first)
                last = jnp.where(mine, roll(strip, 8 * i - 64), last)
            ylo[f, NX + group] = first[0:4]
            yhi[f, NX + group] = last[4:8]


def strips_all(flags, own, from_low, from_high, strips, elo, ehi, *, count):
    lane, row = lanes(), rows()
    low_ok, high_ok = flags[2], flags[3]
    under = (lane < 8) & (row >= 4)
    over = ((lane >> 3) == 9) & (row < 4)
    for f in range(count):
        for group in range(2):
            below = from_low[f, NX + group] * low_ok
            above = from_high[f, NX + group] * high_ok
            below = jnp.concatenate([below, below], axis=0)
            above = jnp.concatenate([above, above], axis=0)
            for i in range(16):
                x = group * 16 + i
                strip = jnp.where(under, roll(below, -8 * i), own[f, x])
                strips[f, x] = jnp.where(over, roll(above, 72 - 8 * i), strip)
        for d in range(DEEP):
            for out, x in ((elo, d), (ehi, NX - DEEP + d)):
                out[f, d, 0:4, :] = from_low[f, x] * low_ok
                out[f, d, 4:8, :] = from_high[f, x] * high_ok
                out[f, d, 8:16, :] = strips[f, x]


def assemble(flags, f, main, strip, own, strips, ylo, yhi, xlo, xhi, elo, ehi):
    def plane(x):
        main[x + DEEP, ROW : ROW + NY, :] = own[f, x]
        main[x + DEEP, ROW - 4 : ROW, :] = ylo[f, x] * flags[2]
        main[x + DEEP, ROW + NY : ROW + NY + 4, :] = yhi[f, x] * flags[3]
        strip[x + DEEP] = strips[f, x]

    grouped(0, NX, 4, plane)
    for slab, edge, at, ok in ((xlo, elo, 0, flags[0]), (xhi, ehi, DEEP + NX, flags[1])):
        for d in range(DEEP):
            main[at + d, ROW : ROW + NY, :] = slab[f, d] * ok
            main[at + d, ROW - 4 : ROW, :] = edge[f, d, 0:4, :] * ok
            main[at + d, ROW + NY : ROW + NY + 4, :] = edge[f, d, 4:8, :] * ok
            strip[at + d] = edge[f, d, 8:16, :] * ok


def near_z(main, sums, start, stop, row, rows, near):
    def several(x):
        block = main[pl.ds(x, size), row : row + rows, :].reshape(size * rows, NZ)
        total = jnp.dot(split(block, 2), near, preferred_element_type=jnp.float32)
        sums[pl.ds(x, size)] = total.reshape(size, rows, NZ)

    groups = -(-(stop - start) // GROUP_DOT)
    size = -(-(stop - start) // groups)

    def step(i, _):
        several(jnp.minimum(start + i * size, stop - size))
        return 0

    lax.fori_loop(0, groups, step, 0)


def ends_z(strip, t, ends):
    return jnp.where(ends, roll(strip, -(8 * t + 4)), 0.0)


def near_xy(main, x, t):
    at = 8 + 8 * t
    rows_y = main[x, at - 1 : at + 7, :] + main[x, at + 1 : at + 9, :]
    rows_x = main[x - 1, at : at + 8, :] + main[x + 1, at : at + 8, :]
    return rows_y + rows_x


def near_sum_strip(strip, x, edge, lane, row):
    here = strip[x]
    left = jnp.where((lane & 7) == 4, edge, roll(here, 1))
    right = jnp.where((lane & 7) == 3, edge, roll(here, -1))
    up = roll(here, -1, 0)
    up = jnp.where(row == 7, roll(up, -8), up)
    down = roll(here, 1, 0)
    down = jnp.where(row == 0, roll(down, 8), down)
    return (up + down) + (strip[x - 1] + strip[x + 1]) + (left + right), here


def react_step(d0, d1, u0, u1, s0, s1, k, g, r):
    kk = k * k
    over = jnp.maximum(k + u0, 0.5)
    inverse = pl.reciprocal(over, approx=True)
    inverse = inverse * (2.0 - over * inverse)
    q = (r * u0) * (u0 * inverse)
    n0 = u0 + (d0 * (kk * s0 - g * u0) - q)
    n1 = u1 + (d1 * (kk * s1 - g * u1) + q)
    return n0, n1


def advance(*refs, first, last):
    refs = list(refs)
    take = lambda n: [refs.pop(0) for _ in range(n)]
    flags, diffusion = take(2)
    own, strips, ylo, yhi, xlo, xhi, elo, ehi = halo = take(8)
    if not first:
        k_main, g_main, r_main, k_strip, g_strip, r_strip = take(6)
    if last:
        (conc,) = take(1)
        (out,) = take(1)
    else:
        out, out_xlo, out_xhi, right, left = take(5)
    if first:
        k_main, g_main, r_main, k_strip, g_strip, r_strip = take(6)
    a_main, b_main, a_strip, b_strip, edges, near = take(6)

    lane, row = lanes(), rows()
    zero = jnp.zeros((8, 128), jnp.float32)
    ends = (lane == 0) | (lane == 127)
    beside = zeros_and_ones("near", 2)
    d0, d1 = diffusion[0], diffusion[1]
    for f in range(2):
        assemble(flags, f, a_main.at[f], a_strip.at[f], *halo)
    if first:
        assemble(flags, 2, k_main, k_strip, *halo)
        assemble(flags, 3, r_main, r_strip, *halo)

        near_z(k_main, near.at[0], 1, XF - 1, 8, 8 * TILES, beside)

        def weigh(x):
            edge, strip = zero, k_strip[x]
            for t in range(TILES):
                at = pl.ds(8 + 8 * t, 8)
                here = k_main[x, at, :]
                total = near_xy(k_main, x, t) + (near[0, x, 8 * t : 8 * t + 8, :] + ends_z(strip, t, ends))
                g_main[x, at, :] = here * total
                edge = jnp.where((lane >> 3) == t, roll(here, 8 * t + 4), edge)
            edges[0, x] = edge

        def weigh_strip(x):
            total, here = near_sum_strip(k_strip, x, edges[0, x], lane, row)
            g_strip[x] = here * total

        grouped(1, XF - 1, GROUP, weigh)
        grouped(1, XF - 1, GROUP_STRIPS, weigh_strip)

    for s in range(1, DEEP + 1):
        src, dst = (a_main, b_main) if s % 2 else (b_main, a_main)
        src_strip, dst_strip = (a_strip, b_strip) if s % 2 else (b_strip, a_strip)
        ending = s == DEEP

        tiles = range(1, TILES - 1) if ending else range(TILES)

        def plane(x):
            edge, strip = [zero, zero], [src_strip[0, x], src_strip[1, x]]
            for t in tiles:
                at = pl.ds(8 + 8 * t, 8)
                there = pl.ds(8 * t, 8)
                u0, u1 = src[0, x, at, :], src[1, x, at, :]
                s0 = near_xy(src.at[0], x, t) + (near[0, x, there, :] + ends_z(strip[0], t, ends))
                s1 = near_xy(src.at[1], x, t) + (near[1, x, there, :] + ends_z(strip[1], t, ends))
                k, r = k_main[x, at, :], r_main[x, at, :]
                new = react_step(d0, d1, u0, u1, s0, s1, k, g_main[x, at, :], r)
                for f in range(2):
                    if not ending:
                        dst[f, x, at, :] = new[f]
                        edge[f] = jnp.where((lane >> 3) == t, roll((u0, u1)[f], 8 * t + 4), edge[f])
                    elif last:
                        was = conc[f, x - DEEP, 8 * (t - 1) : 8 * t, :]
                        out[f, x - DEEP, 8 * (t - 1) : 8 * t, :] = jnp.where(k > 0, new[f] / jnp.maximum(k, 0.5), was)
                    else:
                        out[f, x - DEEP, 8 * (t - 1) : 8 * t, :] = new[f]
                        edge[f] = jnp.where((lane >> 3) == t, roll(new[f], 8 * t + 4), edge[f])
            if not (ending and last):
                for f in range(2):
                    edges[f, x] = edge[f]

        def plane_strips(x):
            s0, u0 = near_sum_strip(src_strip.at[0], x, edges[0, x], lane, row)
            s1, u1 = near_sum_strip(src_strip.at[1], x, edges[1, x], lane, row)
            new = react_step(d0, d1, u0, u1, s0, s1, k_strip[x], g_strip[x], r_strip[x])
            for f in range(2):
                dst_strip[f, x] = new[f]

        for f in range(2):
            near_z(src.at[f], near.at[f], s, XF - s, 8, 8 * TILES, beside)
        grouped(s, XF - s, GROUP, plane)
        if not ending:
            grouped(s, XF - s, GROUP_STRIPS, plane_strips)

    if not last:

        for f in range(2):
            out_xlo[f] = out[f, 0:DEEP]
            out_xhi[f] = out[f, NX - DEEP : NX]
        pack_strips(edges, right, left, 2, DEEP)


def grouped(start, stop, size, work):
    def several(i, _):
        first = jnp.minimum(start + i * size, stop - size)
        for j in range(size):
            work(first + j)
        return 0

    lax.fori_loop(0, -(-(stop - start) // size), several, 0)


def call(kernel, outs, scratch, args, smem, name):
    f32 = lambda shape: jax.ShapeDtypeStruct(shape, jnp.float32)
    return pl.pallas_call(
        kernel,
        out_shape=[f32(shape) for shape in outs],
        in_specs=[SMEM] * smem + [VMEM] * (len(args) - smem),
        out_specs=[VMEM] * len(outs),
        scratch_shapes=[pltpu.VMEM(shape, jnp.float32) for shape in scratch],
        compiler_params=pltpu.CompilerParams(vmem_limit_bytes=LIMIT),
        name=name,
    )(*args)


def shards(concentrations, pore, permeability, rate, diffusion):
    place = []
    for axis in ("gx", "gy", "gz"):
        index = lax.axis_index(axis)
        place += [index > 0, index < lax.axis_size(axis) - 1]
    flags = jnp.stack(place).astype(jnp.float32)

    own, xlo, xhi, right, left = call(
        prepare,
        [(4, NX, NY, NZ)] + [(4, DEEP, NY, NZ)] * 2 + [(4, NX // 2, 8, 128)] * 2,
        [(4, NX, 8, 128)],
        (concentrations, pore, permeability, rate),
        0,
        "prepare",
    )
    rock = ()
    rounds = STEPS // DEEP
    for turn in range(rounds):
        first, last = turn == 0, turn == rounds - 1
        count = 4 if first else 2
        from_xlo, from_xhi = ring(xhi, "gx", 1), ring(xlo, "gx", -1)
        from_left, from_right = ring(right, "gz", 1), ring(left, "gz", -1)
        strips, ylo, yhi = call(
            functools.partial(strips_in, count=count),
            [(count, NX, 8, 128)] + [(count, NX + 2, 4, NZ)] * 2,
            [],
            (flags, own, from_left, from_right),
            1,
            "strips_in",
        )
        from_ylo, from_yhi = ring(yhi, "gy", 1), ring(ylo, "gy", -1)
        strips, elo, ehi = call(
            functools.partial(strips_all, count=count),
            [(count, NX, 8, 128)] + [(count, DEEP, 16, NZ)] * 2,
            [],
            (flags, strips, from_ylo, from_yhi),
            1,
            "strips_all",
        )
        from_elo, from_ehi = ring(ehi, "gx", 1), ring(elo, "gx", -1)
        args = (flags, diffusion, own, strips, from_ylo, from_yhi, from_xlo, from_xhi, from_elo, from_ehi, *rock)
        outs = [(2, NX, NY, NZ)]
        if last:
            args += (concentrations,)
        else:
            outs += [(2, DEEP, NY, NZ)] * 2 + [(2, NX // 2, 8, 128)] * 2
        if first:
            outs += [(XF, YF, NZ)] * 3 + [(XF, 8, 128)] * 3
        scratch = [(2, XF, YF, NZ)] * 2 + [(2, XF, 8, 128)] * 3 + [(2, XF, 8 * TILES, NZ)]
        results = call(functools.partial(advance, first=first, last=last), outs, scratch, args, 2, "advance")
        if last:
            return results[0]
        own, xlo, xhi, right, left = results[:5]
        if first:
            rock = tuple(results[5:])


def solution(mesh):
    placed = (
        P(None, "gx", "gy", "gz"),
        P("gx", "gy", "gz"),
        P("gx", "gy", "gz"),
        P("gx", "gy", "gz"),
        P(),
    )
    return jax.shard_map(
        shards, mesh=mesh, in_specs=placed, out_specs=P(None, "gx", "gy", "gz"), check_vma=False
    )
```

time: 960 us -> 250 us (0.26)
  local copies, waits for them, and re-layouts: 366 us -> 10.7 us
  starting transfers between devices: 333 us -> 70.5 us
  other arithmetic: 252 us -> 0.01 us
  Pallas kernels: 0 us -> 113 us
  waiting for transfers between devices: 0.27 us -> 53.5 us
    ppermute x102 -> x32, starting transfers between devices: 333 us -> 70.5 us  [ring(): lax.ppermute(block, axis, [(i, (i + distance) % size) for i in range(size)])]
    slice x152 -> x0, local copies, waits for them, and re-layouts: 261 us -> none  [the longest x48 134 us: beside(): up = jnp.where(place == count - 1, upper, jnp.roll(fields, -1, axis=dim))]
    mul x17 -> x0, other arithmetic: 177 us -> none  [the longest x16 173 us: single_step(): flux = conduct[None] * flux]
    pallas_call x0 -> x13, Pallas kernels: none -> 113 us  [call(): pl.pallas_call(kernel, out_shape=[f32(shape) for shape in outs], in_specs...]
    another operation x16 -> x1, local copies, waits for them, and re-layouts: 73.4 us -> 0.1 us  [shards(): flags = jnp.stack(place).astype(jnp.float32)]
    ppermute x102 -> x32, waiting for transfers between devices: 0.27 us -> 53.5 us  [ring(): lax.ppermute(block, axis, [(i, (i + distance) % size) for i in range(size)])]
    sub x16 -> x0, other arithmetic: 30.4 us -> none  [single_step(): new_acid = acid + diffusion[0] * flux[0] - reacted]
    broadcast_in_dim x32 -> x0, local copies, waits for them, and re-layouts: 27.2 us -> none  [the longest x16 13.6 us: beside(): down = jnp.where(place == 0, lower, jnp.roll(fields, 1, axis=dim))]
  transfers between devices with their start and end apart: 102 -> 32, of which waited for: 0 -> 15; matrix products, arithmetic and copies ran while one was open for 33% -> 0% of each run, Pallas kernels for 0% -> 3%
where the time goes in v1:
time: 250 us; the launch traced here: 248 us
  Pallas kernels  113 us (45%)
  starting transfers between devices  70.5 us (28%)
  waiting for transfers between devices  53.5 us (21%)
  local copies, waits for them, and re-layouts  10.7 us (4%)
    pallas_call x13, Pallas kernels, call(): pl.pallas_call(kernel, out_shape=[f32(shape) for shape in outs], in_specs...  113 us
    ppermute x32, starting transfers between devices, ring(): lax.ppermute(block, axis, [(i, (i + distance) % size) for i in range(size)])  70.5 us
    ppermute x32, waiting for transfers between devices, ring(): lax.ppermute(block, axis, [(i, (i + distance) % size) for i in range(size)])  53.5 us
    unnamed x18, local copies, waits for them, and re-layouts  10.6 us
  transfers between devices with their start and end apart: 32, of which 15 were waited for; matrix products, arithmetic and copies ran while one was open for 0% of the time, Pallas kernels for 3%

profile of v1, /device:TPU:0, one launch (start us, length us, event | category | flops | bytes accessed | tf_op | source)
XLA Modules:
  0.0 248.1 jit_solution(13832625070001329332)
XLA Ops:
  0.0 1.2 copy-done.5
  1.2 1.2 copy-done.6
  2.5 1.2 copy-done.7
  3.7 5.7 %prepare.1 = (f32[4,32,64,128]{3,2,1,0:T(8,128)}, f32[4,4,64,128]{3,2,1,0:T(8,128)S(1)}, f32[4,4,64,128]{3,2,1,0:T(8,128)S(1)}, f32[4,16,8,128]{3,2,1,0:T(8,128)S(1)}, f32[4,16,8,128]{3,2,1,0:T(8,128)S(1)}) custom-call(f32[2,32,64,128]{3,2,1,0:T(8,128)} %refs_16_.1, s32[32,64,128]{2,1,0:T(8,128)S(1)} %copy-done.5, f32[32,64,128]{2,1,0:T(8,128)S(1)} %copy-done.6, ...), custom_call_target="tpu_custom_call" | custom-call | tf_op jit(solution)/shard_map/prepare/pallas_call | solution.py:318
  9.4 1.7 collective-permute-start.1
  11.1 4.0 %collective-permute-start.4 = (f32[4,4,64,128]{3,2,1,0:T(8,128)S(1)}, f32[4,4,64,128]{3,2,1,0:T(8,128)S(1)}, u32[]{:S(2)}, u32[]{:S(2)}) collective-permute-start(f32[4,4,64,128]{3,2,1,0:T(8,128)S(1)} %get-tuple-element.62), channel_id=1, source_target_pairs={{0,16},{16,32},{32,48},{48,64},{64,80},{80,96},{96,112},{112,0},{1... | collective-permute-start | bytes 1572872 | tf_op jit(solution)/shard_map/ppermute | solution.py:39
  15.1 2.5 collective-permute-start.5
  17.7 11.4 %collective-permute-done.1.from_right = f32[4,16,8,128]{3,2,1,0:T(8,128)S(1)} collective-permute-done((f32[4,16,8,128]{3,2,1,0:T(8,128)S(1)}, f32[4,16,8,128]{3,2,1,0:T(8,128)S(1)}, u32[]{:S(2)}, u32[]{:S(2)}) %collective-permute-start.1) | collective-permute-done | bytes 262176 | tf_op jit(solution)/shard_map/ppermute | solution.py:39
  29.1 2.2 copy-done.1
  31.3 1.0 strips_in.4
  32.3 1.6 collective-permute-start.2
  33.8 1.8 collective-permute-start.3
  35.6 6.1 %collective-permute-done.2.from_low.refs_4_ = f32[4,34,4,128]{3,2,1,0:T(4,128)S(1)} collective-permute-done((f32[4,34,4,128]{3,2,1,0:T(4,128)S(1)}, f32[4,34,4,128]{3,2,1,0:T(4,128)S(1)}, u32[]{:S(2)}, u32[]{:S(2)}) %collective-permute-start.2) | collective-permute-done | bytes 278560 | tf_op jit(solution)/shard_map/ppermute | solution.py:39
  43.1 4.0 %collective-permute-start.6 = (f32[4,4,16,128]{3,2,1,0:T(8,128)S(1)}, f32[4,4,16,128]{3,2,1,0:T(8,128)S(1)}, u32[]{:S(2)}, u32[]{:S(2)}) collective-permute-start(f32[4,4,16,128]{3,2,1,0:T(8,128)S(1)} %get-tuple-element.64), channel_id=1, source_target_pairs={{0,16},{16,32},{32,48},{48,64},{64,80},{80,96},{96,112},{112,0},{1... | collective-permute-start | bytes 393224 | tf_op jit(solution)/shard_map/ppermute | solution.py:39
  47.2 3.2 %collective-permute-start.7 = (f32[4,4,16,128]{3,2,1,0:T(8,128)S(1)}, f32[4,4,16,128]{3,2,1,0:T(8,128)S(1)}, u32[]{:S(2)}, u32[]{:S(2)}) collective-permute-start(f32[4,4,16,128]{3,2,1,0:T(8,128)S(1)} %get-tuple-element.65), channel_id=1, source_target_pairs={{0,112},{16,0},{32,16},{48,32},{64,48},{80,64},{96,80},{112,96},{1... | collective-permute-start | bytes 393224 | tf_op jit(solution)/shard_map/ppermute | solution.py:39
  50.4 3.8 %collective-permute-done.6.refs_8_ = f32[4,4,16,128]{3,2,1,0:T(8,128)S(1)} collective-permute-done((f32[4,4,16,128]{3,2,1,0:T(8,128)S(1)}, f32[4,4,16,128]{3,2,1,0:T(8,128)S(1)}, u32[]{:S(2)}, u32[]{:S(2)}) %collective-permute-start.6) | collective-permute-done | bytes 131104 | tf_op jit(solution)/shard_map/ppermute | solution.py:39
  54.3 2.7 %collective-permute-done.7.refs_9_ = f32[4,4,16,128]{3,2,1,0:T(8,128)S(1)} collective-permute-done((f32[4,4,16,128]{3,2,1,0:T(8,128)S(1)}, f32[4,4,16,128]{3,2,1,0:T(8,128)S(1)}, u32[]{:S(2)}, u32[]{:S(2)}) %collective-permute-start.7) | collective-permute-done | bytes 131104 | tf_op jit(solution)/shard_map/ppermute | solution.py:39
  57.0 28.6 %advance.4 = (f32[2,32,64,128]{3,2,1,0:T(8,128)}, f32[2,4,64,128]{3,2,1,0:T(8,128)S(1)}, f32[2,4,64,128]{3,2,1,0:T(8,128)S(1)}, f32[2,16,8,128]{3,2,1,0:T(8,128)...) custom-call(f32[6]{0:T(128)S(1)} %convert_element_type.3.flags.refs_, ...), custom_call_target="tpu_custom_call" | custom-call | tf_op jit(solution)/shard_map/advance/pallas_call | solution.py:318
  85.6 1.7 collective-permute-start.9
  88.1 4.8 %collective-permute-start.13 = (f32[2,4,64,128]{3,2,1,0:T(8,128)S(1)}, f32[2,4,64,128]{3,2,1,0:T(8,128)S(1)}, u32[]{:S(2)}, u32[]{:S(2)}) collective-permute-start(f32[2,4,64,128]{3,2,1,0:T(8,128)S(1)} %get-tuple-element.74), channel_id=1, source_target_pairs={{0,112},{16,0},{32,16},{48,32},{64,48},{80,64},{96,80},{112,96},{1... | collective-permute-start | bytes 786440 | tf_op jit(solution)/shard_map/ppermute | solution.py:39
  92.9 3.9 %collective-permute-done.9.from_right = f32[2,16,8,128]{3,2,1,0:T(8,128)S(1)} collective-permute-done((f32[2,16,8,128]{3,2,1,0:T(8,128)S(1)}, f32[2,16,8,128]{3,2,1,0:T(8,128)S(1)}, u32[]{:S(2)}, u32[]{:S(2)}) %collective-permute-start.9) | collective-permute-done | bytes 131104 | tf_op jit(solution)/shard_map/ppermute | solution.py:39
  96.8 1.6 copy-done.2
  99.3 1.6 collective-permute-start.10
  100.8 1.8 collective-permute-start.11
  102.6 4.4 %collective-permute-done.10.from_low.refs_4_ = f32[2,34,4,128]{3,2,1,0:T(4,128)S(1)} collective-permute-done((f32[2,34,4,128]{3,2,1,0:T(4,128)S(1)}, f32[2,34,4,128]{3,2,1,0:T(4,128)S(1)}, u32[]{:S(2)}, u32[]{:S(2)}) %collective-permute-start.10) | collective-permute-done | bytes 139296 | tf_op jit(solution)/shard_map/ppermute | solution.py:39
  108.0 5.6 %collective-permute-start.15 = (f32[2,4,16,128]{3,2,1,0:T(8,128)S(1)}, f32[2,4,16,128]{3,2,1,0:T(8,128)S(1)}, u32[]{:S(2)}, u32[]{:S(2)}) collective-permute-start(f32[2,4,16,128]{3,2,1,0:T(8,128)S(1)} %get-tuple-element.76), channel_id=1, source_target_pairs={{0,112},{16,0},{32,16},{48,32},{64,48},{80,64},{96,80},{112,96},{1... | collective-permute-start | bytes 196616 | tf_op jit(solution)/shard_map/ppermute | solution.py:39
  113.6 2.2 collective-permute-done.14.refs_8_
  115.9 24.4 %advance.5 = (f32[2,32,64,128]{3,2,1,0:T(8,128)}, f32[2,4,64,128]{3,2,1,0:T(8,128)S(1)}, f32[2,4,64,128]{3,2,1,0:T(8,128)S(1)}, f32[2,16,8,128]{3,2,1,0:T(8,128)S(1)}, f32[2,16,8,128]{3,2,1,0:T(8,128)S(1)}) custom-call(f32[6]{0:T(128)S(1)} %convert_element_type.3.flags.refs_0_, f32[2]{0:T(128)S(1)} %copy-done.8, ...), custom_call_target="tpu_custom_call" | custom-call | tf_op jit(solution)/shard_map/advance/pallas_call | solution.py:318
  140.2 1.7 collective-permute-start.17
  142.0 5.6 %collective-permute-start.21 = (f32[2,4,64,128]{3,2,1,0:T(8,128)S(1)}, f32[2,4,64,128]{3,2,1,0:T(8,128)S(1)}, u32[]{:S(2)}, u32[]{:S(2)}) collective-permute-start(f32[2,4,64,128]{3,2,1,0:T(8,128)S(1)} %get-tuple-element.91), channel_id=1, source_target_pairs={{0,112},{16,0},{32,16},{48,32},{64,48},{80,64},{96,80},{112,96},{1... | collective-permute-start | bytes 786440 | tf_op jit(solution)/shard_map/ppermute | solution.py:39
  147.6 3.9 %collective-permute-done.17.from_right = f32[2,16,8,128]{3,2,1,0:T(8,128)S(1)} collective-permute-done((f32[2,16,8,128]{3,2,1,0:T(8,128)S(1)}, f32[2,16,8,128]{3,2,1,0:T(8,128)S(1)}, u32[]{:S(2)}, u32[]{:S(2)}) %collective-permute-start.17) | collective-permute-done | bytes 131104 | tf_op jit(solution)/shard_map/ppermute | solution.py:39
  151.5 1.6 copy-done.3
  154.0 1.2 collective-permute-start.18
  155.2 2.1 collective-permute-start.19
  157.3 3.0 %collective-permute-done.18.from_low.refs_4_ = f32[2,34,4,128]{3,2,1,0:T(4,128)S(1)} collective-permute-done((f32[2,34,4,128]{3,2,1,0:T(4,128)S(1)}, f32[2,34,4,128]{3,2,1,0:T(4,128)S(1)}, u32[]{:S(2)}, u32[]{:S(2)}) %collective-permute-start.18) | collective-permute-done | bytes 139296 | tf_op jit(solution)/shard_map/ppermute | solution.py:39
  161.1 6.5 %collective-permute-start.23 = (f32[2,4,16,128]{3,2,1,0:T(8,128)S(1)}, f32[2,4,16,128]{3,2,1,0:T(8,128)S(1)}, u32[]{:S(2)}, u32[]{:S(2)}) collective-permute-start(f32[2,4,16,128]{3,2,1,0:T(8,128)S(1)} %get-tuple-element.93), channel_id=1, source_target_pairs={{0,112},{16,0},{32,16},{48,32},{64,48},{80,64},{96,80},{112,96},{1... | collective-permute-start | bytes 196616 | tf_op jit(solution)/shard_map/ppermute | solution.py:39
  167.7 2.2 collective-permute-done.22.refs_8_
  169.8 24.3 %advance.6 = (f32[2,32,64,128]{3,2,1,0:T(8,128)}, f32[2,4,64,128]{3,2,1,0:T(8,128)S(1)}, f32[2,4,64,128]{3,2,1,0:T(8,128)S(1)}, f32[2,16,8,128]{3,2,1,0:T(8,128)S(1)}, f32[2,16,8,128]{3,2,1,0:T(8,128)S(1)}) custom-call(f32[6]{0:T(128)S(1)} %convert_element_type.3.flags.refs_0_, f32[2]{0:T(128)S(1)} %copy-done.8, ...), custom_call_target="tpu_custom_call" | custom-call | tf_op jit(solution)/shard_map/advance/pallas_call | solution.py:318
  194.2 1.7 collective-permute-start.25
  195.9 5.7 %collective-permute-start.29 = (f32[2,4,64,128]{3,2,1,0:T(8,128)S(1)}, f32[2,4,64,128]{3,2,1,0:T(8,128)S(1)}, u32[]{:S(2)}, u32[]{:S(2)}) collective-permute-start(f32[2,4,64,128]{3,2,1,0:T(8,128)S(1)} %get-tuple-element.102), channel_id=1, source_target_pairs={{0,112},{16,0},{32,16},{48,32},{64,48},{80,64},{96,80},{112,96},{1... | collective-permute-start | bytes 786440 | tf_op jit(solution)/shard_map/ppermute | solution.py:39
  201.6 3.1 %collective-permute-done.24.from_left = f32[2,16,8,128]{3,2,1,0:T(8,128)S(1)} collective-permute-done((f32[2,16,8,128]{3,2,1,0:T(8,128)S(1)}, f32[2,16,8,128]{3,2,1,0:T(8,128)S(1)}, u32[]{:S(2)}, u32[]{:S(2)}) %collective-permute-start.24) | collective-permute-done | bytes 131104 | tf_op jit(solution)/shard_map/ppermute | solution.py:39
  204.7 1.6 copy-done.4
  207.1 1.8 collective-permute-start.26
  208.8 1.8 collective-permute-start.27
  210.6 3.7 %collective-permute-done.26.from_low.refs_4_ = f32[2,34,4,128]{3,2,1,0:T(4,128)S(1)} collective-permute-done((f32[2,34,4,128]{3,2,1,0:T(4,128)S(1)}, f32[2,34,4,128]{3,2,1,0:T(4,128)S(1)}, u32[]{:S(2)}, u32[]{:S(2)}) %collective-permute-start.26) | collective-permute-done | bytes 139296 | tf_op jit(solution)/shard_map/ppermute | solution.py:39
  215.2 7.1 %collective-permute-start.31 = (f32[2,4,16,128]{3,2,1,0:T(8,128)S(1)}, f32[2,4,16,128]{3,2,1,0:T(8,128)S(1)}, u32[]{:S(2)}, u32[]{:S(2)}) collective-permute-start(f32[2,4,16,128]{3,2,1,0:T(8,128)S(1)} %get-tuple-element.104), channel_id=1, source_target_pairs={{0,112},{16,0},{32,16},{48,32},{64,48},{80,64},{96,80},{112,96},{1... | collective-permute-start | bytes 196616 | tf_op jit(solution)/shard_map/ppermute | solution.py:39
  222.2 2.2 collective-permute-done.30.refs_8_
  224.4 23.6 %advance.7 = f32[2,32,64,128]{3,2,1,0:T(8,128)} custom-call(f32[6]{0:T(128)S(1)} %convert_element_type.3.flags.refs_0_, f32[2]{0:T(128)S(1)} %copy-done.8, f32[2,32,64,128]{3,2,1,0:T(8,128)} %get-tuple-element.94.fields.refs_2_, f32[2,32,8,128]{3,2,1,0:T(8,128)S(1)} %get-tuple-element.100.refs_3_, ...), custom_call_target="tpu_custom_call" | custom-call | tf_op jit(solution)/shard_map/advance/pallas_call | solution.py:318
  (49 shorter events, 7.6 us)
Async XLA Ops:
  0.0 1.2 copy-start.5
  1.2 1.2 copy-start.6
  2.5 1.2 copy-start.7
  9.4 8.3 %collective-permute-start = (f32[4,16,8,128]{3,2,1,0:T(8,128)S(1)}, f32[4,16,8,128]{3,2,1,0:T(8,128)S(1)}, u32[]{:S(2)}, u32[]{:S(2)}) collective-permute-start(f32[4,16,8,128]{3,2,1,0:T(8,128)S(1)} %get-tuple-element.56), channel_id=1, source_target_pairs={{0,1},{1,2},{2,3},{3,0},{4,5},{5,6},{6,7},{7,4},{8,9},{9,10},{10,1... | collective-permute-start | bytes 786440 | tf_op jit(solution)/shard_map/ppermute | solution.py:39
  9.4 19.7 %collective-permute-start.1 = (f32[4,16,8,128]{3,2,1,0:T(8,128)S(1)}, f32[4,16,8,128]{3,2,1,0:T(8,128)S(1)}, u32[]{:S(2)}, u32[]{:S(2)}) collective-permute-start(f32[4,16,8,128]{3,2,1,0:T(8,128)S(1)} %get-tuple-element.57), channel_id=1, source_target_pairs={{0,3},{1,0},{2,1},{3,2},{4,7},{5,4},{6,5},{7,6},{8,11},{9,8},{10,9... | collective-permute-start | bytes 786440 | tf_op jit(solution)/shard_map/ppermute | solution.py:39
  11.1 39.3 %collective-permute-start.4 = (f32[4,4,64,128]{3,2,1,0:T(8,128)S(1)}, f32[4,4,64,128]{3,2,1,0:T(8,128)S(1)}, u32[]{:S(2)}, u32[]{:S(2)}) collective-permute-start(f32[4,4,64,128]{3,2,1,0:T(8,128)S(1)} %get-tuple-element.62), channel_id=1, source_target_pairs={{0,16},{16,32},{32,48},{48,64},{64,80},{80,96},{96,112},{112,0},{1... | collective-permute-start | bytes 1572872 | tf_op jit(solution)/shard_map/ppermute | solution.py:39
  15.1 35.3 %collective-permute-start.5 = (f32[4,4,64,128]{3,2,1,0:T(8,128)S(1)}, f32[4,4,64,128]{3,2,1,0:T(8,128)S(1)}, u32[]{:S(2)}, u32[]{:S(2)}) collective-permute-start(f32[4,4,64,128]{3,2,1,0:T(8,128)S(1)} %get-tuple-element.63), channel_id=1, source_target_pairs={{0,112},{16,0},{32,16},{48,32},{64,48},{80,64},{96,80},{112,96},{1... | collective-permute-start | bytes 1572872 | tf_op jit(solution)/shard_map/ppermute | solution.py:39
  29.1 2.2 copy-start.1
  31.3 25.7 %copy-start.8 = (f32[2]{0:T(128)S(1)}, f32[2]{0:T(128)}, u32[]{:S(2)}) copy-start(f32[2]{0:T(128)} %refs_1_.7) | copy-start | bytes 28
  32.3 9.4 %collective-permute-start.2 = (f32[4,34,4,128]{3,2,1,0:T(4,128)S(1)}, f32[4,34,4,128]{3,2,1,0:T(4,128)S(1)}, u32[]{:S(2)}, u32[]{:S(2)}) collective-permute-start(f32[4,34,4,128]{3,2,1,0:T(4,128)S(1)} %get-tuple-element.59), channel_id=1, source_target_pairs={{0,4},{4,8},{8,12},{12,0},{1,5},{5,9},{9,13},{13,1},{2,6},{6,10},{... | collective-permute-start | bytes 835592 | tf_op jit(solution)/shard_map/ppermute | solution.py:39
  33.8 8.4 %collective-permute-start.3 = (f32[4,34,4,128]{3,2,1,0:T(4,128)S(1)}, f32[4,34,4,128]{3,2,1,0:T(4,128)S(1)}, u32[]{:S(2)}, u32[]{:S(2)}) collective-permute-start(f32[4,34,4,128]{3,2,1,0:T(4,128)S(1)} %get-tuple-element.60), channel_id=1, source_target_pairs={{0,12},{4,0},{8,4},{12,8},{1,13},{5,1},{9,5},{13,9},{2,14},{6,2},{... | collective-permute-start | bytes 835592 | tf_op jit(solution)/shard_map/ppermute | solution.py:39
  43.1 11.1 %collective-permute-start.6 = (f32[4,4,16,128]{3,2,1,0:T(8,128)S(1)}, f32[4,4,16,128]{3,2,1,0:T(8,128)S(1)}, u32[]{:S(2)}, u32[]{:S(2)}) collective-permute-start(f32[4,4,16,128]{3,2,1,0:T(8,128)S(1)} %get-tuple-element.64), channel_id=1, source_target_pairs={{0,16},{16,32},{32,48},{48,64},{64,80},{80,96},{96,112},{112,0},{1... | collective-permute-start | bytes 393224 | tf_op jit(solution)/shard_map/ppermute | solution.py:39
  47.2 9.8 %collective-permute-start.7 = (f32[4,4,16,128]{3,2,1,0:T(8,128)S(1)}, f32[4,4,16,128]{3,2,1,0:T(8,128)S(1)}, u32[]{:S(2)}, u32[]{:S(2)}) collective-permute-start(f32[4,4,16,128]{3,2,1,0:T(8,128)S(1)} %get-tuple-element.65), channel_id=1, source_target_pairs={{0,112},{16,0},{32,16},{48,32},{64,48},{80,64},{96,80},{112,96},{1... | collective-permute-start | bytes 393224 | tf_op jit(solution)/shard_map/ppermute | solution.py:39
  85.5 7.4 %collective-permute-start.8 = (f32[2,16,8,128]{3,2,1,0:T(8,128)S(1)}, f32[2,16,8,128]{3,2,1,0:T(8,128)S(1)}, u32[]{:S(2)}, u32[]{:S(2)}) collective-permute-start(f32[2,16,8,128]{3,2,1,0:T(8,128)S(1)} %get-tuple-element.67), channel_id=1, source_target_pairs={{0,1},{1,2},{2,3},{3,0},{4,5},{5,6},{6,7},{7,4},{8,9},{9,10},{10,1... | collective-permute-start | bytes 393224 | tf_op jit(solution)/shard_map/ppermute | solution.py:39
  85.6 11.2 %collective-permute-start.9 = (f32[2,16,8,128]{3,2,1,0:T(8,128)S(1)}, f32[2,16,8,128]{3,2,1,0:T(8,128)S(1)}, u32[]{:S(2)}, u32[]{:S(2)}) collective-permute-start(f32[2,16,8,128]{3,2,1,0:T(8,128)S(1)} %get-tuple-element.68), channel_id=1, source_target_pairs={{0,3},{1,0},{2,1},{3,2},{4,7},{5,4},{6,5},{7,6},{8,11},{9,8},{10,9... | collective-permute-start | bytes 393224 | tf_op jit(solution)/shard_map/ppermute | solution.py:39
  87.3 26.3 %collective-permute-start.12 = (f32[2,4,64,128]{3,2,1,0:T(8,128)S(1)}, f32[2,4,64,128]{3,2,1,0:T(8,128)S(1)}, u32[]{:S(2)}, u32[]{:S(2)}) collective-permute-start(f32[2,4,64,128]{3,2,1,0:T(8,128)S(1)} %get-tuple-element.73), channel_id=1, source_target_pairs={{0,16},{16,32},{32,48},{48,64},{64,80},{80,96},{96,112},{112,0},{1... | collective-permute-start | bytes 786440 | tf_op jit(solution)/shard_map/ppermute | solution.py:39
  88.1 25.5 %collective-permute-start.13 = (f32[2,4,64,128]{3,2,1,0:T(8,128)S(1)}, f32[2,4,64,128]{3,2,1,0:T(8,128)S(1)}, u32[]{:S(2)}, u32[]{:S(2)}) collective-permute-start(f32[2,4,64,128]{3,2,1,0:T(8,128)S(1)} %get-tuple-element.74), channel_id=1, source_target_pairs={{0,112},{16,0},{32,16},{48,32},{64,48},{80,64},{96,80},{112,96},{1... | collective-permute-start | bytes 786440 | tf_op jit(solution)/shard_map/ppermute | solution.py:39
  96.8 1.6 copy-start.2
  99.3 7.8 %collective-permute-start.10 = (f32[2,34,4,128]{3,2,1,0:T(4,128)S(1)}, f32[2,34,4,128]{3,2,1,0:T(4,128)S(1)}, u32[]{:S(2)}, u32[]{:S(2)}) collective-permute-start(f32[2,34,4,128]{3,2,1,0:T(4,128)S(1)} %get-tuple-element.70), channel_id=1, source_target_pairs={{0,4},{4,8},{8,12},{12,0},{1,5},{5,9},{9,13},{13,1},{2,6},{6,10},{... | collective-permute-start | bytes 417800 | tf_op jit(solution)/shard_map/ppermute | solution.py:39
  100.8 6.3 %collective-permute-start.11 = (f32[2,34,4,128]{3,2,1,0:T(4,128)S(1)}, f32[2,34,4,128]{3,2,1,0:T(4,128)S(1)}, u32[]{:S(2)}, u32[]{:S(2)}) collective-permute-start(f32[2,34,4,128]{3,2,1,0:T(4,128)S(1)} %get-tuple-element.71), channel_id=1, source_target_pairs={{0,12},{4,0},{8,4},{12,8},{1,13},{5,1},{9,5},{13,9},{2,14},{6,2},{... | collective-permute-start | bytes 417800 | tf_op jit(solution)/shard_map/ppermute | solution.py:39
  107.9 7.9 %collective-permute-start.14 = (f32[2,4,16,128]{3,2,1,0:T(8,128)S(1)}, f32[2,4,16,128]{3,2,1,0:T(8,128)S(1)}, u32[]{:S(2)}, u32[]{:S(2)}) collective-permute-start(f32[2,4,16,128]{3,2,1,0:T(8,128)S(1)} %get-tuple-element.75), channel_id=1, source_target_pairs={{0,16},{16,32},{32,48},{48,64},{64,80},{80,96},{96,112},{112,0},{1... | collective-permute-start | bytes 196616 | tf_op jit(solution)/shard_map/ppermute | solution.py:39
  108.0 7.9 %collective-permute-start.15 = (f32[2,4,16,128]{3,2,1,0:T(8,128)S(1)}, f32[2,4,16,128]{3,2,1,0:T(8,128)S(1)}, u32[]{:S(2)}, u32[]{:S(2)}) collective-permute-start(f32[2,4,16,128]{3,2,1,0:T(8,128)S(1)} %get-tuple-element.76), channel_id=1, source_target_pairs={{0,112},{16,0},{32,16},{48,32},{64,48},{80,64},{96,80},{112,96},{1... | collective-permute-start | bytes 196616 | tf_op jit(solution)/shard_map/ppermute | solution.py:39
  140.2 7.4 %collective-permute-start.16 = (f32[2,16,8,128]{3,2,1,0:T(8,128)S(1)}, f32[2,16,8,128]{3,2,1,0:T(8,128)S(1)}, u32[]{:S(2)}, u32[]{:S(2)}) collective-permute-start(f32[2,16,8,128]{3,2,1,0:T(8,128)S(1)} %get-tuple-element.84), channel_id=1, source_target_pairs={{0,1},{1,2},{2,3},{3,0},{4,5},{5,6},{6,7},{7,4},{8,9},{9,10},{10,1... | collective-permute-start | bytes 393224 | tf_op jit(solution)/shard_map/ppermute | solution.py:39
  140.2 11.3 %collective-permute-start.17 = (f32[2,16,8,128]{3,2,1,0:T(8,128)S(1)}, f32[2,16,8,128]{3,2,1,0:T(8,128)S(1)}, u32[]{:S(2)}, u32[]{:S(2)}) collective-permute-start(f32[2,16,8,128]{3,2,1,0:T(8,128)S(1)} %get-tuple-element.85), channel_id=1, source_target_pairs={{0,3},{1,0},{2,1},{3,2},{4,7},{5,4},{6,5},{7,6},{8,11},{9,8},{10,9... | collective-permute-start | bytes 393224 | tf_op jit(solution)/shard_map/ppermute | solution.py:39
  142.0 25.7 %collective-permute-start.20 = (f32[2,4,64,128]{3,2,1,0:T(8,128)S(1)}, f32[2,4,64,128]{3,2,1,0:T(8,128)S(1)}, u32[]{:S(2)}, u32[]{:S(2)}) collective-permute-start(f32[2,4,64,128]{3,2,1,0:T(8,128)S(1)} %get-tuple-element.90), channel_id=1, source_target_pairs={{0,16},{16,32},{32,48},{48,64},{64,80},{80,96},{96,112},{112,0},{1... | collective-permute-start | bytes 786440 | tf_op jit(solution)/shard_map/ppermute | solution.py:39
  142.0 25.7 %collective-permute-start.21 = (f32[2,4,64,128]{3,2,1,0:T(8,128)S(1)}, f32[2,4,64,128]{3,2,1,0:T(8,128)S(1)}, u32[]{:S(2)}, u32[]{:S(2)}) collective-permute-start(f32[2,4,64,128]{3,2,1,0:T(8,128)S(1)} %get-tuple-element.91), channel_id=1, source_target_pairs={{0,112},{16,0},{32,16},{48,32},{64,48},{80,64},{96,80},{112,96},{1... | collective-permute-start | bytes 786440 | tf_op jit(solution)/shard_map/ppermute | solution.py:39
  151.5 1.6 copy-start.3
  154.0 6.3 %collective-permute-start.18 = (f32[2,34,4,128]{3,2,1,0:T(4,128)S(1)}, f32[2,34,4,128]{3,2,1,0:T(4,128)S(1)}, u32[]{:S(2)}, u32[]{:S(2)}) collective-permute-start(f32[2,34,4,128]{3,2,1,0:T(4,128)S(1)} %get-tuple-element.87), channel_id=1, source_target_pairs={{0,4},{4,8},{8,12},{12,0},{1,5},{5,9},{9,13},{13,1},{2,6},{6,10},{... | collective-permute-start | bytes 417800 | tf_op jit(solution)/shard_map/ppermute | solution.py:39
  155.2 5.1 %collective-permute-start.19 = (f32[2,34,4,128]{3,2,1,0:T(4,128)S(1)}, f32[2,34,4,128]{3,2,1,0:T(4,128)S(1)}, u32[]{:S(2)}, u32[]{:S(2)}) collective-permute-start(f32[2,34,4,128]{3,2,1,0:T(4,128)S(1)} %get-tuple-element.88), channel_id=1, source_target_pairs={{0,12},{4,0},{8,4},{12,8},{1,13},{5,1},{9,5},{13,9},{2,14},{6,2},{... | collective-permute-start | bytes 417800 | tf_op jit(solution)/shard_map/ppermute | solution.py:39
  161.0 8.8 %collective-permute-start.22 = (f32[2,4,16,128]{3,2,1,0:T(8,128)S(1)}, f32[2,4,16,128]{3,2,1,0:T(8,128)S(1)}, u32[]{:S(2)}, u32[]{:S(2)}) collective-permute-start(f32[2,4,16,128]{3,2,1,0:T(8,128)S(1)} %get-tuple-element.92), channel_id=1, source_target_pairs={{0,16},{16,32},{32,48},{48,64},{64,80},{80,96},{96,112},{112,0},{1... | collective-permute-start | bytes 196616 | tf_op jit(solution)/shard_map/ppermute | solution.py:39
  161.1 8.7 %collective-permute-start.23 = (f32[2,4,16,128]{3,2,1,0:T(8,128)S(1)}, f32[2,4,16,128]{3,2,1,0:T(8,128)S(1)}, u32[]{:S(2)}, u32[]{:S(2)}) collective-permute-start(f32[2,4,16,128]{3,2,1,0:T(8,128)S(1)} %get-tuple-element.93), channel_id=1, source_target_pairs={{0,112},{16,0},{32,16},{48,32},{64,48},{80,64},{96,80},{112,96},{1... | collective-permute-start | bytes 196616 | tf_op jit(solution)/shard_map/ppermute | solution.py:39
  194.2 30.3 %copy-start = (f32[40,96,128]{2,1,0:T(8,128)S(1)}, f32[40,96,128]{2,1,0:T(8,128)}, u32[]{:S(2)}) copy-start(f32[40,96,128]{2,1,0:T(8,128)} %get-tuple-element.78.refs_11_) | copy-start | bytes 5898244
  194.2 10.5 %collective-permute-start.24 = (f32[2,16,8,128]{3,2,1,0:T(8,128)S(1)}, f32[2,16,8,128]{3,2,1,0:T(8,128)S(1)}, u32[]{:S(2)}, u32[]{:S(2)}) collective-permute-start(f32[2,16,8,128]{3,2,1,0:T(8,128)S(1)} %get-tuple-element.95), channel_id=1, source_target_pairs={{0,1},{1,2},{2,3},{3,0},{4,5},{5,6},{6,7},{7,4},{8,9},{9,10},{10,1... | collective-permute-start | bytes 393224 | tf_op jit(solution)/shard_map/ppermute | solution.py:39
  194.2 10.5 %collective-permute-start.25 = (f32[2,16,8,128]{3,2,1,0:T(8,128)S(1)}, f32[2,16,8,128]{3,2,1,0:T(8,128)S(1)}, u32[]{:S(2)}, u32[]{:S(2)}) collective-permute-start(f32[2,16,8,128]{3,2,1,0:T(8,128)S(1)} %get-tuple-element.96), channel_id=1, source_target_pairs={{0,3},{1,0},{2,1},{3,2},{4,7},{5,4},{6,5},{7,6},{8,11},{9,8},{10,9... | collective-permute-start | bytes 393224 | tf_op jit(solution)/shard_map/ppermute | solution.py:39
  195.9 26.3 %collective-permute-start.28 = (f32[2,4,64,128]{3,2,1,0:T(8,128)S(1)}, f32[2,4,64,128]{3,2,1,0:T(8,128)S(1)}, u32[]{:S(2)}, u32[]{:S(2)}) collective-permute-start(f32[2,4,64,128]{3,2,1,0:T(8,128)S(1)} %get-tuple-element.101), channel_id=1, source_target_pairs={{0,16},{16,32},{32,48},{48,64},{64,80},{80,96},{96,112},{112,0},{1... | collective-permute-start | bytes 786440 | tf_op jit(solution)/shard_map/ppermute | solution.py:39
  195.9 26.3 %collective-permute-start.29 = (f32[2,4,64,128]{3,2,1,0:T(8,128)S(1)}, f32[2,4,64,128]{3,2,1,0:T(8,128)S(1)}, u32[]{:S(2)}, u32[]{:S(2)}) collective-permute-start(f32[2,4,64,128]{3,2,1,0:T(8,128)S(1)} %get-tuple-element.102), channel_id=1, source_target_pairs={{0,112},{16,0},{32,16},{48,32},{64,48},{80,64},{96,80},{112,96},{1... | collective-permute-start | bytes 786440 | tf_op jit(solution)/shard_map/ppermute | solution.py:39
  204.7 1.6 copy-start.4
  207.1 7.3 %collective-permute-start.26 = (f32[2,34,4,128]{3,2,1,0:T(4,128)S(1)}, f32[2,34,4,128]{3,2,1,0:T(4,128)S(1)}, u32[]{:S(2)}, u32[]{:S(2)}) collective-permute-start(f32[2,34,4,128]{3,2,1,0:T(4,128)S(1)} %get-tuple-element.98), channel_id=1, source_target_pairs={{0,4},{4,8},{8,12},{12,0},{1,5},{5,9},{9,13},{13,1},{2,6},{6,10},{... | collective-permute-start | bytes 417800 | tf_op jit(solution)/shard_map/ppermute | solution.py:39
  208.8 5.5 %collective-permute-start.27 = (f32[2,34,4,128]{3,2,1,0:T(4,128)S(1)}, f32[2,34,4,128]{3,2,1,0:T(4,128)S(1)}, u32[]{:S(2)}, u32[]{:S(2)}) collective-permute-start(f32[2,34,4,128]{3,2,1,0:T(4,128)S(1)} %get-tuple-element.99), channel_id=1, source_target_pairs={{0,12},{4,0},{8,4},{12,8},{1,13},{5,1},{9,5},{13,9},{2,14},{6,2},{... | collective-permute-start | bytes 417800 | tf_op jit(solution)/shard_map/ppermute | solution.py:39
  215.1 9.3 %collective-permute-start.30 = (f32[2,4,16,128]{3,2,1,0:T(8,128)S(1)}, f32[2,4,16,128]{3,2,1,0:T(8,128)S(1)}, u32[]{:S(2)}, u32[]{:S(2)}) collective-permute-start(f32[2,4,16,128]{3,2,1,0:T(8,128)S(1)} %get-tuple-element.103), channel_id=1, source_target_pairs={{0,16},{16,32},{32,48},{48,64},{64,80},{80,96},{96,112},{112,0},{1... | collective-permute-start | bytes 196616 | tf_op jit(solution)/shard_map/ppermute | solution.py:39
  215.2 9.2 %collective-permute-start.31 = (f32[2,4,16,128]{3,2,1,0:T(8,128)S(1)}, f32[2,4,16,128]{3,2,1,0:T(8,128)S(1)}, u32[]{:S(2)}, u32[]{:S(2)}) collective-permute-start(f32[2,4,16,128]{3,2,1,0:T(8,128)S(1)} %get-tuple-element.104), channel_id=1, source_target_pairs={{0,112},{16,0},{32,16},{48,32},{64,48},{80,64},{96,80},{112,96},{1... | collective-permute-start | bytes 196616 | tf_op jit(solution)/shard_map/ppermute | solution.py:39
